TPU v7x, 32 devices: a whole 2x2x4 slice. The times are simulated.
32 devices in a mesh: gy: 4 (over y, x), gx: 8 (over z, core).
Axes of the slice: x: 2, y: 2, z: 4, core: 2. Of those that a mesh axis runs over, the one named last changes fastest.
Arguments:
- features: bfloat16 [128, 1024, 256], P('gy', 'gx'), may hold values from -8 to 8
- tissue: int32 [8, 64], P('gy', 'gx'), may hold values 0 or 1
- owner_map: int32 [4, 8, 16, 1], P('gy', 'gx'), may hold values from 0 to 7; in each aligned block of 16 rows (0 to 15, 16 to 31, ..., all dimensions but the last counted through in order) at most 2 rows name the same one
- w_conv: bfloat16 [9, 256, 256], replicated, may hold values from -0.125 to 0.125
- w_stride: bfloat16 [4, 256, 256], replicated, may hold values from -0.1875 to 0.1875
- w_query: float32 [256, 256], replicated, may hold values from -0.375 to 0.375
- w_key: float32 [256, 256], replicated, may hold values from -0.375 to 0.375
- w_value: float32 [256, 256], replicated, may hold values from -0.375 to 0.375
- cotangent: float32 [256], replicated, may hold values from -6 to 6
Outputs:
- embedding: float32 [256], replicated
- input_grad: bfloat16 [128, 1024, 256], P('gy', 'gx')
- conv_grad: float32 [9, 256, 256], replicated
Inputs may be any that keep to these rules, and one draw needn't show every extreme that they name: `owner_map`: among the tiles of one device, no owner index is named more than 2 times.
All inputs are finite; a program needn't handle non-finite values. No bound on the sum of `tissue` on one device may be relied on, other than what follows from the above.
Results may differ from a plain program's by a relative error of at most 0.017.
Values may be sent and summed in bfloat16 or wider, within the bound.
No kernel may reach another device: no remote copies, remote signals or barrier semaphores. Data moves between devices by JAX's collectives and lax.ppermute only.
A program may use at most 128 MiB of HBM per device.

v0:
```python
import math

import jax
import jax.numpy as jnp
from jax import lax
from jax.experimental import pallas as pl
from jax.experimental.pallas import tpu as pltpu
from jax.sharding import Mesh, PartitionSpec as P

HEADS = 4
F32 = jnp.float32
BF16 = jnp.bfloat16

attention_bias = -1.0
loss_scale = 512.0

ROWS = 32
COLS = 128
CH = 256
HALO = 48
LANES = 128
STEP = 5
TILE_CELLS = 64


def shape(dims, dtype):
    return jax.ShapeDtypeStruct(dims, dtype)


def nt(left, right):
    return lax.dot_general(left, right, (((1,), (1,)), ((), ())), preferred_element_type=F32)


def tn(left, right):
    return lax.dot_general(left, right, (((0,), (0,)), ((), ())), preferred_element_type=F32)


def nn(left, right):
    return jnp.dot(left, right, preferred_element_type=F32)


def halves(value):
    high = value.astype(BF16)
    return high, (value - high.astype(F32)).astype(BF16)


def wide_product(product, left, right):
    (a, b), (c, d) = left, right
    return product(a, c) + (product(a, d) + product(b, c))


def half_product(product, left, right):
    left = left.astype(BF16)
    return product(left, right[0]) + product(left, right[1])


def iota(dims, axis):
    return lax.broadcasted_iota(jnp.int32, dims, axis)


def gate_of(value):
    return 0.5 * jnp.tanh(0.5 * value) + 0.5


def is_odd(axis):
    return lax.axis_index(axis) % 2 == 1


def order_body(first_ref, last_ref, even_ref, odd_ref):
    order_rows(first_ref[0], last_ref[0], even_ref, odd_ref)


def columns_body(block, left_ref, right_ref):
    row, spot = iota((HALO, ROWS * 16), 0), iota((HALO, ROWS * 16), 1)
    for out, at, place in ((left_ref, 0, 0), (right_ref, COLS - 16, 15)):
        pick = (spot == (row - 1) * 16 + place).astype(F32).astype(BF16)
        out[...] = nn(pick, block[:, at : at + 16].reshape(ROWS * 16, CH)).astype(BF16)


def corner_body(left, right, even, odd, top_ref, bot_ref, even_ref, odd_ref):
    low = is_odd("gy")
    top_ref[0] = jnp.where(low, even[0], odd[0])
    bot_ref[0] = jnp.where(low, odd[0], even[0])
    row = iota((HALO, CH), 0)
    whole = []
    for side, at in ((left, 0), (right, COLS - 16)):
        part = slice(0, 1) if at == 0 else slice(15, 16)
        above = top_ref[0, at : at + 16].astype(F32)[part]
        below = bot_ref[0, at : at + 16].astype(F32)[part]
        whole.append(jnp.where(row == 0, above, jnp.where(row == ROWS + 1, below, side[...].astype(F32))))
    high = is_odd("core")
    even_ref[...] = jnp.where(high, whole[0], whole[1]).astype(BF16)
    odd_ref[...] = jnp.where(high, whole[1], whole[0]).astype(BF16)


def sides(even, odd):
    high = is_odd("core")
    one, two = even[...].astype(F32), odd[...].astype(F32)
    return jnp.where(high, one, two), jnp.where(high, two, one)


def forward_taps(weight, b):
    return jnp.concatenate([weight[3 * a + b] for a in range(3)], axis=0)


HALF = ROWS // 2
BLOCKS = (HALF - 1) // STEP
PARTS = (2, 2, 2, 2, 2, 2, 2, 1)


def with_first(wide, value):
    start = jnp.where(iota((8, wide.shape[1]), 0) == 0, value, wide[0:8])
    return jnp.concatenate([start, wide[8:]], axis=0)


def with_last(wide, value):
    end = jnp.where(iota((8, wide.shape[1]), 0) == 7, value, wide[COLS - 8 :])
    return jnp.concatenate([wide[: COLS - 8], end], axis=0)


def neighbours(row):
    wide = row.astype(F32)
    left = with_first(pltpu.roll(wide, 1, 0), 0.0)
    right = with_last(pltpu.roll(wide, COLS - 1, 0), 0.0)
    return left.astype(BF16), right.astype(BF16)


HALVES = (slice(0, LANES), slice(LANES, CH))


def silu_pair(value, half_mask):
    half = 0.5 * value
    bend = jnp.tanh(half)
    kept = (1.0 + bend) * half_mask
    return value * kept, kept * (1.0 + half * (1.0 - bend))


def forward_body(flags_ref, feat, weight, slope_ref, sums, cols, wide, prod_a, prod_b, *, band):
    sums[...] = jnp.zeros_like(sums)
    base = (HALF - 1) * band
    halves_of_mask = [0.5 * flags_ref[band, tile].astype(F32) for tile in range(8)]

    def build(i):
        here = slice(i * COLS, (i + 1) * COLS)
        for lanes in HALVES:
            left, right = neighbours(feat[base + i, :, lanes])
            wide[here, lanes] = left
            wide[here, lanes.start + CH : lanes.stop + CH] = right

    def around(start, count):
        taken = []
        for a in range(3):
            here = slice((start + a) * COLS, (start + a + count) * COLS)
            rows = feat[base + start + a : base + start + a + count].reshape(count * COLS, CH)
            taken += [wide[here, 0:CH], rows, wide[here, CH:]]
        return jnp.concatenate(taken, axis=1)

    def finish(r, prod, first):
        at = r - HALF * band
        for tile in range(8):
            here = slice(16 * tile, 16 * tile + 16)
            value = prod[first + 16 * tile : first + 16 * tile + 16]
            pixel = feat[r, here].astype(F32)
            bent, slope = silu_pair(value, halves_of_mask[tile])
            summed = pixel + bent
            slope_ref[at, here] = slope.astype(BF16)
            sums[r % 2, here] += summed
            if tile in (0, 7):
                edge = slice(0, 1) if tile == 0 else slice(15, 16)
                for i, part in enumerate((value, summed, pixel)):
                    cols[2 * i + tile // 7, at : at + 1] = part[edge]

    prods = (prod_a, prod_b)
    parts = PARTS
    built, done = parts[0] + 2, 0
    for i in range(built):
        build(i)
    for block in range(len(parts) + 1):
        start = sum(parts[:block])
        if block < len(parts):
            prods[block % 2][0 : parts[block] * COLS] = nn(
                around(start, parts[block]), weight[...].reshape(9 * CH, CH)
            )
        ahead = min(HALF + 1, sum(parts[: block + 2]) + 2)
        for j in range(STEP):
            if done < start:
                finish(base + 1 + done, prods[(block - 1) % 2], (done - sum(parts[: block - 1])) * COLS)
                done += 1
            if built < ahead:
                build(built)
                built += 1


def border_body(
    flags_ref, feat, weight, sums_a, sums_b, cols_a, cols_b, top, bot, even, odd, strided, owner_ref,
    pooled_ref, token_ref, edge_ref, side_ref, side32,
):
    added = []
    cols = [jnp.concatenate([cols_a[i], cols_b[i]], axis=0) for i in range(6)]
    for i, whole in enumerate(sides(even, odd)):
        side32[...] = whole
        near = [side32[a : a + ROWS].astype(BF16) for a in range(3)]
        added.append(nn(jnp.concatenate(near, axis=1), forward_taps(weight, 2 * i)))

    def pair(one, two):
        return jnp.concatenate([one, two], axis=0)

    taken = jnp.concatenate(
        [pair(top[0], feat[ROWS - 2]), pair(feat[0], feat[ROWS - 1]), pair(feat[1], bot[0])], axis=1
    )
    low, mid, high = (nn(taken, forward_taps(weight, b)) for b in range(3))
    rows = []
    for i, r in enumerate((0, ROWS - 1)):
        part = slice(i * COLS, (i + 1) * COLS)
        before = with_first(pltpu.roll(low[part], 1, 0), added[0][r : r + 1])
        after = with_last(pltpu.roll(high[part], COLS - 1, 0), added[1][r : r + 1])
        value = mid[part] + before + after
        keep = jnp.concatenate(
            [0.5 * jnp.full((16, CH), flags_ref[i, t], jnp.int32).astype(F32) for t in range(8)], axis=0
        )
        bent, slope = silu_pair(value, keep)
        edge_ref[i] = slope.astype(BF16)
        rows.append(feat[r].astype(F32) + bent)

    line = iota((ROWS, CH), 0)
    deltas = []
    for i in range(2):
        tile = 7 * i
        keep = 0.5 * jnp.where(line < ROWS // 2, flags_ref[0, tile], flags_ref[1, tile]).astype(F32)
        bent, side_ref[i] = silu_pair(cols[i] + added[i], keep)
        inside = (line > 0) & (line < ROWS - 1)
        deltas.append(jnp.where(inside, cols[4 + i] + bent - cols[2 + i], 0.0))

    row, spot = iota((16, COLS), 0), iota((16, COLS), 1)
    pick = ((spot // 16 == row % 8) & (spot % 2 == row // 8)).astype(F32).astype(BF16)
    place = iota((16, CH), 0)
    parts = {}
    for band in range(2):
        for a in range(2):
            total = (sums_a, sums_b)[band][a]
            if band == a:
                total += rows[band]
            high, low = halves(total)
            part = nn(pick, high) + nn(pick, low)
            mine = (line // 16 == band) & (line % 2 == a)
            for i in range(2):
                delta = jnp.sum(jnp.where(mine, deltas[i], 0.0), axis=0, keepdims=True)
                part += jnp.where(place == 15 * i, delta, 0.0)
            parts[band, a] = part
    taken = [
        jnp.concatenate([parts[band, a][8 * b : 8 * b + 8] for band in range(2)], axis=0)
        for a in range(2)
        for b in range(2)
    ]
    high, low = halves(jnp.concatenate(taken, axis=1))
    flat = strided[...].reshape(4 * CH, CH)
    pooled = (nn(high, flat) + nn(low, flat)) * (1.0 / TILE_CELLS)
    pooled_ref[...] = pooled
    normed = pooled * lax.rsqrt(jnp.mean(pooled * pooled, axis=-1, keepdims=True) + 1e-05)
    token_ref[:, 0:CH] = normed.astype(BF16)
    owner = jnp.full((16, LANES), -1, jnp.int32)
    for tile in range(16):
        named = jnp.where(flags_ref[tile // 8, tile % 8] != 0, owner_ref[tile], -1)
        owner = jnp.where(iota((16, LANES), 0) == tile, named, owner)
    token_ref[:, CH:] = (owner == iota((16, LANES), 1)).astype(F32).astype(BF16)


def turn_body(feat, top, bot, w_query, w_key, w_value, token, turned_ref, high_ref, low_ref):
    turned_ref[:, 0:COLS] = top[0].T
    turned_ref[:, (ROWS + 1) * COLS :] = bot[0].T

    @pl.loop(0, ROWS // 4)
    def _(i):
        for j in range(4):
            here = pl.multiple_of((4 * i + j + 1) * COLS, COLS)
            turned_ref[:, pl.ds(here, COLS)] = feat[4 * i + j].T

    for i, one in enumerate((w_query, w_key, w_value)):
        high, low = halves(one[...])
        high_ref[:, i * CH : (i + 1) * CH] = high
        low_ref[:, i * CH : (i + 1) * CH] = low


def attention_body(
    mine, other, pooled_ref, high_w, low_w, cot, strided, spread_ref, emb_ref, band, grad_ref, *, seed_scale
):
    gz, core = lax.axis_index("gz"), lax.axis_index("core")

    def rows_of(depth, other):
        return pl.ds(pl.multiple_of(depth * 32 + other * 16, 16), 16)

    for k in range(mine.shape[0]):
        depth = lax.bitwise_xor(gz, k)
        band[rows_of(depth, core)] = mine[k]
        band[rows_of(depth, 1 - core)] = other[k]
    count = band.shape[0]
    tokens, group = band[:, 0:CH], band[:, CH:]
    pair = nt(group, group)
    pairs = jnp.concatenate([pair] * HEADS, axis=0)
    projected = nn(tokens, high_w[...]) + nn(tokens, low_w[...])
    query, key, value = (projected[:, i * CH : (i + 1) * CH] for i in range(3))
    lane = iota((1, CH), 1) // (CH // HEADS)
    scale = 1.0 / math.sqrt(CH // HEADS)

    def by_head(array):
        return jnp.concatenate([jnp.where(lane == h, array, 0.0) for h in range(HEADS)], axis=0)

    queries, keys = halves(by_head(query)), halves(by_head(key))
    gate = gate_of(wide_product(nt, queries, halves(key)) * scale + attention_bias)
    weights = gate * pairs
    seed = cot[...] * seed_scale
    seeds = jnp.where(lane == iota((8, CH), 0), seed, 0.0)
    values = halves(value)
    along = wide_product(nt, halves(seeds), values)
    columns, grads = [], []
    for h in range(HEADS):
        part = slice(h * count, (h + 1) * count)
        columns.append(jnp.sum(weights[part], axis=0, keepdims=True))
        grads.append(weights[part] * (1.0 - gate[part]) * (along[h : h + 1] * scale))
    columns = halves(jnp.concatenate(columns + [jnp.zeros((8 - HEADS, count), F32)], axis=0))
    grad_ref[:, 0:CH] = half_product(nn, jnp.concatenate(grads, axis=1), keys)
    grad_ref[:, CH : 2 * CH] = half_product(tn, jnp.concatenate(grads, axis=0), queries)
    grad_ref[:, 2 * CH :] = half_product(tn, columns[0], halves(seeds))
    mixed = wide_product(nn, columns, values)
    mixed = jnp.sum(jnp.where(lane == iota((8, CH), 0), mixed, 0.0), axis=0, keepdims=True)
    high = mixed.astype(BF16).astype(F32)
    low = mixed - high
    rows = iota((16, LANES), 0)
    packed = jnp.zeros((16, LANES), F32)
    for i, part in enumerate((high[:, :LANES], high[:, LANES:], low[:, :LANES], low[:, LANES:])):
        packed = jnp.where(rows == i, part, packed)
    emb_ref[...] = packed.astype(BF16)

    grad = half_product(nt, grad_ref[rows_of(gz, core)], (high_w[...], low_w[...]))
    grad = grad.astype(BF16).astype(F32)
    pooled = pooled_ref[...]
    inv = lax.rsqrt(jnp.mean(pooled * pooled, axis=-1, keepdims=True) + 1e-05)
    unit = pooled * inv
    back = inv * (grad - unit * jnp.mean(grad * unit, axis=-1, keepdims=True))
    cell = (back * (1.0 / TILE_CELLS)).astype(BF16)
    spot, row = iota((COLS, 16), 0), iota((COLS, 16), 1)
    expand = ((spot // 16 == row % 8) & (spot % 2 == row // 8)).astype(F32).astype(BF16)
    taps = nt(cell, strided[...].reshape(4 * CH, CH))
    for band in range(2):
        here = taps[8 * band : 8 * band + 8]
        both = [
            jnp.concatenate([here[:, (2 * a + b) * CH : (2 * a + b + 1) * CH] for a in range(2)], axis=1)
            for b in range(2)
        ]
        high, low = halves(jnp.concatenate(both, axis=0))
        spread = nn(expand, high) + nn(expand, low)
        for a in range(2):
            spread_ref[band * 2 + a] = spread[:, a * CH : (a + 1) * CH]


GROUPS = (4, 12, 16)


def weight_body(
    spread, slope_a, slope_b, edge, side, turned, even, odd,
    wide, keep_ref, give_ref, even_ref, odd_ref, left_ref, right_ref, total, first, last,
):
    first[...] = jnp.zeros_like(first)
    last[...] = jnp.zeros_like(last)

    def build(r):
        if r in (0, ROWS - 1):
            slope = edge[r // HALF].astype(F32)
        else:
            slope = (slope_a, slope_b)[r // HALF][r % HALF].astype(F32)
            slope = with_last(with_first(slope, side[0, r : r + 1]), side[1, r : r + 1])
        grad = (spread[(r // HALF) * 2 + r % 2] * slope).astype(BF16)
        here = slice(r * COLS, (r + 1) * COLS)
        wide[here, 2 * CH :], wide[here, 0:CH] = neighbours(grad)
        wide[here, CH : 2 * CH] = grad
        full = grad.astype(F32)
        for a in range(3):
            first[a, r + a : r + a + 1] = full[0:1]
            last[a, r + a : r + a + 1] = full[COLS - 1 :]

    is_one = is_odd("core")
    left, right = (part.astype(BF16) for part in sides(even, odd))

    def put(part, a, b):
        if b == 0:
            part += tn(left, first[a].astype(BF16))
        if b == 2:
            part += tn(right, last[a].astype(BF16))
        low, high = part[:, :LANES], part[:, LANES:]
        at = slice((3 * a + b) * CH, (3 * a + b + 1) * CH)
        keep_ref[at] = jnp.where(is_one, high, low).astype(BF16)
        give_ref[at] = jnp.where(is_one, low, high).astype(BF16)

    for r in range(GROUPS[0]):
        build(r)
    start = 0
    for g, count in enumerate(GROUPS):
        here = slice(start * COLS, (start + count) * COLS)
        near = [turned[:, (start + a) * COLS : (start + a + count) * COLS] for a in range(3)]
        near = jnp.concatenate(near, axis=0)
        start += count
        ahead = GROUPS[g + 1] if g + 1 < len(GROUPS) else 0
        for b in range(3):
            part = slice(b * CH, (b + 1) * CH)
            result = nn(near, wide[here, part])
            if g > 0:
                result += total[:, part]
            if ahead:
                total[:, part] = result
            for r in range(ahead * b // 3, ahead * (b + 1) // 3):
                build(start + r)
            if not ahead:
                for a in range(3):
                    put(result[a * CH : (a + 1) * CH], a, b)

    centre = slice(CH, 2 * CH)
    order_rows(wide[0:COLS, centre], wide[(ROWS - 1) * COLS :, centre], even_ref, odd_ref)
    left_ref[...] = first[1].astype(BF16)
    right_ref[...] = last[1].astype(BF16)


def order_rows(first, last, even_ref, odd_ref):
    odd = is_odd("gy")
    even_ref[0] = jnp.where(odd, first, last)
    odd_ref[0] = jnp.where(odd, last, first)


def back_taps(weight, taps):
    return jnp.concatenate([weight[tap] for tap in taps], axis=1)


def input_blocks(wide, weight, first, blocks, prods, finish, send=None):
    for block in range(blocks + 1):
        if block < blocks:
            at = first + STEP * block
            near = [wide[(at + step) * COLS : (at + step + STEP) * COLS] for step in (1, 0, -1)]
            prods[block % 2][...] = nt(jnp.concatenate(near, axis=1), back_taps(weight, range(9)))
        if block > 0:
            at = first + STEP * (block - 1)
            for j in range(STEP):
                finish(at + j, prods[(block - 1) % 2][j * COLS : (j + 1) * COLS])
            if send is not None:
                send(at, STEP)


UPPER = 2 * STEP


def upper_body(wide, spread, weight, done, raw_ref, prod_a, prod_b):
    def finish(r, prod):
        value = spread[r % 2] + prod
        done[r - 1] = value.astype(BF16)
        raw_ref[0, r : r + 1] = value[0:1]
        raw_ref[1, r : r + 1] = value[COLS - 1 :]

    input_blocks(wide, weight, 1, UPPER // STEP, (prod_a, prod_b), finish)


def lower_body(
    wide, top, bot, even, odd, spread, weight, upper, raw, out, prod_a, prod_b, side32, added, done, fixed, sems
):
    started = []

    def start(source, target):
        started.append(pltpu.make_async_copy(source, target, sems.at[len(started)]))
        started[-1].start()

    start(upper.at[:, 16 : COLS - 16], out.at[1 : UPPER + 1, 16 : COLS - 16])
    for i, whole in enumerate(sides(even, odd)):
        side32[...] = whole
        near = [side32[2 - a : 2 - a + ROWS].astype(BF16) for a in range(3)]
        taps = back_taps(weight, [3 * a + 2 - 2 * i for a in range(3)])
        added[i] = nt(jnp.concatenate(near, axis=1), taps)

    small = iota((16, CH), 0)
    for i in range(2):
        at = (COLS - 16) * i
        for r in range(1, UPPER + 1):
            value = raw[i, r : r + 1] + added[i, r : r + 1]
            old = upper[r - 1, at : at + 16].astype(F32)
            fixed[i, r - 1] = jnp.where(small == 15 * i, value, old).astype(BF16)
        start(fixed.at[i], out.at[1 : UPPER + 1, at : at + 16])

    def place(r):
        return r - UPPER if r else 0

    def finish(r, prod):
        prod = with_first(prod, prod[0:1] + added[0, r : r + 1])
        prod = with_last(prod, prod[COLS - 1 :] + added[1, r : r + 1])
        done[place(r)] = (spread[(r // HALF) * 2 + r % 2] + prod).astype(BF16)

    def send(first, count):
        start(done.at[place(first) : place(first) + count], out.at[first : first + count])

    input_blocks(wide, weight, UPPER + 1, (ROWS - 2 - UPPER) // STEP, (prod_a, prod_b), finish, send)

    def row(r):
        return wide[r * COLS : (r + 1) * COLS]

    def outside(one):
        left, right = neighbours(one[0])
        return jnp.concatenate([right, one[0], left], axis=1)

    def pair(one, two):
        return jnp.concatenate([one, two], axis=0)

    near = [pair(row(1), outside(bot)), pair(row(0), row(ROWS - 1)), pair(outside(top), row(ROWS - 2))]
    both = nt(jnp.concatenate(near, axis=1), back_taps(weight, range(9)))
    for i, r in enumerate((0, ROWS - 1)):
        finish(r, both[i * COLS : (i + 1) * COLS])
        send(r, 1)
    for one in started:
        one.wait()


def add_up(refs, rows):
    total = refs[0][0:rows].astype(F32)
    for one in refs[1:]:
        total += one[0:rows].astype(F32)
    return total.astype(BF16)


def deal(total_ref, outs, size, axis):
    for k, out in enumerate(reversed(outs)):
        at = lax.bitwise_xor(lax.axis_index(axis), k) * size
        out[0:size] = total_ref[pl.ds(pl.multiple_of(at, 16), size)]


def chip_sum_body(one, two, emb, *refs):
    outs, total_ref = refs[:-1], refs[-1]
    rows = one.shape[0]
    size = rows // len(outs)
    total_ref[...] = add_up((one, two), rows)
    deal(total_ref, outs, size, "gy")
    for out in outs:
        out[size:] = emb[...]


def band_sum_body(*refs, terms, norm_scale):
    outs, emb_ref, total_ref = refs[terms:-2], refs[-2], refs[-1]
    rows = total_ref.shape[0]
    total_ref[...] = add_up(refs[:terms], rows)
    deal(total_ref, outs, rows // len(outs), "gz")
    embs = []
    for one in (refs[0], *refs[terms - 1 : 0 : -1]):
        part = one[rows : rows + 16].astype(F32)
        embs.append(part[0:2] + part[2:4])
    while len(embs) > 1:
        embs = [a + b for a, b in zip(embs[0::2], embs[1::2])]
    emb_ref[:, 0:LANES] = embs[0][0:1] * norm_scale
    emb_ref[:, LANES:] = embs[0][1:2] * norm_scale


def last_sum_body(*refs):
    refs[-1][...] = add_up(refs[:-1], refs[-1].shape[0])


def stack_body(*refs):
    for i, one in enumerate(refs[:-1]):
        refs[-1][i] = one[...]


def half_body(array, *refs, other):
    grad_ref, buf, sems = refs[-3:]
    gy, gz, core = (lax.axis_index(name) for name in ("gy", "gz", "core"))
    bands, depth, share = array.shape[:3]
    half = 1 - core if other else core
    lanes = pl.ds(pl.multiple_of(half * LANES, LANES), LANES)
    started = []
    for k in range(bands):
        first = lax.bitwise_xor(gy, k) * (depth * share)
        for j in range(depth):
            at = first + lax.bitwise_xor(gz, j) * share
            buf[pl.ds(pl.multiple_of(at, 16), share)] = array[k, j].astype(F32) * (1.0 / loss_scale)
        here = pl.ds(pl.multiple_of(first, 16), depth * share)
        started.append(pltpu.make_async_copy(buf.at[here], grad_ref.at[here, lanes], sems.at[k]))
        started[-1].start()
    for one in started:
        one.wait()


SMEM = pl.BlockSpec(memory_space=pltpu.SMEM)
VMEM = pl.BlockSpec(memory_space=pltpu.VMEM)
HBM = pl.BlockSpec(memory_space=pltpu.HBM)


def run(body, args, outs, scratch=(), flops=1 << 20, mib=8, far=(), **rest):
    specs = [HBM if i in far else SMEM if a.dtype == jnp.int32 else VMEM for i, a in enumerate(args)]
    return pl.pallas_call(
        body,
        in_specs=specs,
        out_shape=outs,
        scratch_shapes=list(scratch),
        compiler_params=pltpu.CompilerParams(vmem_limit_bytes=mib << 20),
        cost_estimate=pl.CostEstimate(flops=flops, bytes_accessed=1 << 20, transcendentals=0),
        **rest,
    )(*args)


def per_device(features, tissue, owner_map, w_conv, w_stride, w_query, w_key, w_value, cotangent):
    gy_count, gz_count, cores = lax.axis_size("gy"), lax.axis_size("gz"), lax.axis_size("core")
    gx_count, chips = gz_count * cores, gy_count * gz_count
    across = ("gz", "core")
    norm_scale = 1.0 / math.sqrt(16 * gy_count * gx_count)
    swap = [(i, i ^ 1) for i in range(cores)]

    def pairs(value, axis, count, odd):
        low = range(odd, count - 1, 2)
        return lax.ppermute(value, axis, [(i, i + 1) for i in low] + [(i + 1, i) for i in low])

    def others(values, axis, count):
        got = [
            lax.ppermute(values[k - 1], axis, [(i, i ^ k) for i in range(count)])
            for k in range(count - 1, 0, -1)
        ]
        return got[::-1]

    column = shape((HALO, CH), BF16)
    line = shape((1, COLS, CH), BF16)

    def row_halos(even, odd):
        return pairs(even, "gy", gy_count, 0), pairs(odd, "gy", gy_count, 1)

    def corners(left, right, even, odd):
        return run(corner_body, (left, right, even, odd), [line, line, column, column], mib=1)

    def column_halos(even, odd):
        return pairs(even, across, gx_count, 0), pairs(odd, across, gx_count, 1)

    conv_flops = 2 * ROWS * COLS * 9 * CH * CH
    prod = pltpu.VMEM((STEP * COLS, CH), F32)
    side32 = pltpu.VMEM((HALO, CH), F32)
    half_block = shape((HALF, COLS, CH), BF16)

    def forward(band, weight):
        return run(
            lambda *refs: forward_body(*refs, band=band),
            (tissue, features, weight),
            [half_block, shape((2, COLS, CH), F32), shape((6, HALF, CH), F32)],
            [pltpu.VMEM(((HALF + 1) * COLS, 2 * CH), BF16), prod, prod],
            flops=conv_flops // 2,
            mib=16,
        )

    rows = run(
        order_body, (features[:1], features[ROWS - 1 :]), [line, line], flops=conv_flops, mib=2
    )
    outer = run(columns_body, (features,), [column, column], mib=2)
    even, odd = row_halos(*rows)
    slope_a, sums_a, cols_a = forward(0, w_conv)
    even, odd, cols_a = lax.optimization_barrier((even, odd, cols_a))
    top, bot, even, odd = corners(*outer, even, odd)
    weight_b, even = lax.optimization_barrier((w_conv, even))
    even, odd = column_halos(even, odd)
    slope_b, sums_b, cols_b = forward(1, weight_b)
    pooled, token, edge, side = run(
        border_body,
        (
            tissue, features, w_conv, sums_a, sums_b, cols_a, cols_b, top, bot, even, odd, w_stride,
            owner_map.reshape(16),
        ),
        [
            shape((16, CH), F32),
            shape((16, CH + LANES), BF16),
            shape((2, COLS, CH), BF16),
            shape((2, ROWS, CH), F32),
        ],
        [side32],
        flops=conv_flops // 8,
        mib=12,
    )
    def stacked(terms):
        return run(stack_body, terms, shape((len(terms),) + terms[0].shape, BF16), mib=4)

    turned, high_w, low_w = run(
        turn_body,
        (features, top, bot, w_query, w_key, w_value, token),
        [shape((CH, (ROWS + 2) * COLS), BF16), shape((CH, 3 * CH), BF16), shape((CH, 3 * CH), BF16)],
        flops=conv_flops // 4,
        mib=12,
    )
    tokens = stacked([token] + others([token] * (gz_count - 1), "gz", gz_count))
    tokens, high_w = lax.optimization_barrier((tokens, high_w))
    count = 16 * gx_count
    spread, emb = run(
        lambda *refs: attention_body(*refs, seed_scale=loss_scale * norm_scale),
        (tokens, lax.ppermute(tokens, "core", swap), pooled, high_w, low_w, cotangent.reshape(1, CH), w_stride),
        [shape((4, COLS, CH), F32), shape((16, LANES), BF16)],
        [pltpu.VMEM((count, CH + LANES), BF16), pltpu.VMEM((count, 3 * CH), F32)],
        flops=1 << 30,
        mib=12,
    )
    border = pltpu.VMEM((3, HALO, CH), F32)
    wide, keep, give, *outer = run(
        weight_body,
        (spread, slope_a, slope_b, edge, side, turned, even, odd),
        [
            shape((ROWS * COLS, 3 * CH), BF16),
            shape((9 * CH, LANES), BF16),
            shape((9 * CH, LANES), BF16),
            line,
            line,
            column,
            column,
        ],
        [pltpu.VMEM((3 * CH, 3 * CH), F32), border, border],
        flops=conv_flops,
        mib=20,
    )

    share = -(-9 * CH // (16 * chips)) * 16
    spare = share * chips - 9 * CH
    taken = lax.ppermute(give, "core", swap)
    pre_rows = row_halos(*outer[:2])
    if spare:
        keep, taken = (jnp.pad(a, ((0, spare), (0, 0))) for a in (keep, taken))

    whole_rows = share * chips
    band_rows = share * gz_count
    parts = run(
        chip_sum_body,
        (keep, taken, emb),
        [shape((band_rows + 16, LANES), BF16)] * gy_count,
        [pltpu.VMEM((whole_rows, LANES), BF16)],
        mib=6,
    )[::-1]
    *parts, wide_upper = lax.optimization_barrier((*parts, wide))
    upper, raw = run(
        upper_body,
        (wide_upper, spread, w_conv),
        [shape((UPPER, COLS, CH), BF16), shape((2, HALF, CH), F32)],
        [prod, prod],
        flops=conv_flops // 3,
        mib=12,
    )
    raw, *outer = lax.optimization_barrier((raw, *outer[2:], *pre_rows))
    parts = [parts[0]] + others(parts[1:], "gy", gy_count)[::-1]
    top, bot, even, odd = corners(*outer)
    even, odd = column_halos(even, odd)
    *parts, raw = lax.optimization_barrier((*parts, raw))
    embedding, *parts = run(
        lambda *refs: band_sum_body(*refs, terms=gy_count, norm_scale=norm_scale),
        parts,
        [shape((share, LANES), BF16)] * gz_count + [shape((1, CH), F32)],
        [pltpu.VMEM((band_rows, LANES), BF16)],
        mib=4,
    )[::-1]
    *parts, even, odd = lax.optimization_barrier((*parts, even, odd))
    parts = [parts[0]] + others(parts[1:], "gz", gz_count)[::-1]
    mine = run(last_sum_body, parts, shape((share, LANES), BF16), mib=2)
    row = stacked([mine] + others([mine] * (gz_count - 1), "gz", gz_count))
    row, wide_lower = lax.optimization_barrier((row, wide))
    input_grad = run(
        lower_body,
        (wide_lower, top, bot, even, odd, spread, w_conv, upper, raw),
        shape((ROWS, COLS, CH), BF16),
        [
            prod,
            prod,
            side32,
            pltpu.VMEM((2, ROWS, CH), F32),
            pltpu.VMEM((ROWS - UPPER, COLS, CH), BF16),
            pltpu.VMEM((2, UPPER, 16, CH), BF16),
            pltpu.SemaphoreType.DMA((BLOCKS + 6,)),
        ],
        flops=conv_flops // 2,
        mib=16,
        out_specs=HBM,
    )
    planes = [row] + others([row] * (gy_count - 1), "gy", gy_count)
    *planes, input_grad = lax.optimization_barrier((*planes, input_grad))
    plane = stacked(planes)
    other = lax.ppermute(plane, "core", swap)
    whole = shape((whole_rows, CH), F32)
    buffers = [pltpu.VMEM((whole_rows, LANES), F32), pltpu.SemaphoreType.DMA((gy_count,))]
    half_grad = run(
        lambda *refs: half_body(*refs, other=False), (plane,), whole, buffers, mib=4, out_specs=HBM
    )
    conv_grad = run(
        lambda *refs: half_body(*refs, other=True),
        (other, half_grad),
        whole,
        buffers,
        mib=4,
        far=(1,),
        out_specs=HBM,
        input_output_aliases={1: 0},
    )
    return embedding.reshape(CH), input_grad, conv_grad[: 9 * CH].reshape(9, CH, CH)


def solution(mesh):
    sizes = mesh.devices.shape
    split = Mesh(mesh.devices.reshape(sizes[0], sizes[1] // 2, 2), ("gy", "gz", "core"))
    gx = ("gz", "core")
    in_specs = (P("gy", gx, None), P("gy", gx), P("gy", gx, None, None), P(), P(), P(), P(), P(), P())
    out_specs = (P(), P("gy", gx, None), P())
    return jax.shard_map(per_device, mesh=split, in_specs=in_specs, out_specs=out_specs, check_vma=False)
```

profile of v0, /device:TPU:0, one launch (start us, length us, event | category | flops | bytes accessed | tf_op | source)
XLA Modules:
  0.0 79.4 jit_solution(10032689201347203921)
XLA Ops:
  0.6 0.9 %fusion = (bf16[1,128,256]{2,1,0:T(8,128)(2,1)S(1)}, bf16[1,128,256]{2,1,0:T(8,128)(2,1)S(1)}) fusion(bf16[32,128,256]{2,1,0:T(8,128)(2,1)} %feat.3), kind=kLoop, calls=%fused_computation | loop fusion | bytes 262144 | tf_op jit(solution)/shard_map/slice | solution.py:646
  1.6 3.0 %collective-permute-start = (bf16[1,128,256]{2,1,0:T(8,128)(2,1)S(1)}, bf16[1,128,256]{2,1,0:T(8,128)(2,1)S(1)}, u32[]{:S(2)}, u32[]{:S(2)}) collective-permute-start(bf16[1,128,256]{2,1,0:T(8,128)(2,1)S(1)} %get-tuple-element.86), channel_id=1, source_target_pairs={{0,8},{16,24},{8,0},{24,16},{1,9},{17,25},{9,1},{25,17},{2,10},{18... | collective-permute-start | bytes 196616 | tf_op jit(solution)/shard_map/ppermute | solution.py:609
  4.6 0.7 collective-permute-start.1
  5.3 3.5 %shard_map.112 = (bf16[16,128,256]{2,1,0:T(8,128)(2,1)S(1)}, f32[2,128,256]{2,1,0:T(8,128)S(1)}, f32[6,16,256]{2,1,0:T(8,128)S(1)}) custom-call(s32[2,8]{1,0:T(2,128)S(1)} %copy-done.3, bf16[32,128,256]{2,1,0:T(8,128)(2,1)S(1)} %copy-done.1, bf16[9,256,256]{2,1,0:T(8,128)(2,1)S(1)} %copy-done), custom_call_target="tpu_custom_call" | custom-call | flops 2415919104 | bytes 1048576 | tf_op jit(solution)/shard_map/pallas_call | solution.py:589
  8.8 0.2 shard_map.113
  9.2 1.0 %collective-permute-start.3 = (bf16[48,256]{1,0:T(8,128)(2,1)S(1)}, bf16[48,256]{1,0:T(8,128)(2,1)S(1)}, u32[]{:S(2)}, u32[]{:S(2)}) collective-permute-start(bf16[48,256]{1,0:T(8,128)(2,1)S(1)} %get-tuple-element.99), channel_id=1, source_target_pairs={{1,2},{3,4},{5,6},{2,1},{4,3},{6,5},{9,10},{11,12},{13,14},{10,9},... | collective-permute-start | bytes 73736 | tf_op jit(solution)/shard_map/ppermute | solution.py:609
  10.2 3.5 %shard_map.116 = (bf16[16,128,256]{2,1,0:T(8,128)(2,1)S(1)}, f32[2,128,256]{2,1,0:T(8,128)S(1)}, f32[6,16,256]{2,1,0:T(8,128)S(1)}) custom-call(s32[2,8]{1,0:T(2,128)S(1)} %copy-done.3, bf16[32,128,256]{2,1,0:T(8,128)(2,1)S(1)} %copy-done.1, bf16[9,256,256]{2,1,0:T(8,128)(2,1)S(1)} %copy-done), custom_call_target="tpu_custom_call" | custom-call | flops 2415919104 | bytes 1048576 | tf_op jit(solution)/shard_map/pallas_call | solution.py:589
  13.8 2.0 %shard_map.117 = (f32[16,256]{1,0:T(8,128)S(1)}, bf16[16,384]{1,0:T(8,128)(2,1)S(1)}, bf16[2,128,256]{2,1,0:T(8,128)(2,1)S(1)}, f32[2,32,256]{2,1,0:T(8,128)S(1)}) custom-call(s32[2,8]{1,0:T(2,128)S(1)} %copy-done.3, bf16[32,128,256]{2,1,0:T(8,128)(2,1)S(1)} %copy-done.1, bf16[9,256,256]{2,1,0:T(8,128)(2,1)S(1)} %copy-done, ...), custom_call_target="tpu_custom_call" | custom-call | flops 603979776 | bytes 1048576 | tf_op jit(solution)/shard_map/pallas_call | solution.py:589
  15.8 5.4 %collective-permute-start.6 = (bf16[16,384]{1,0:T(8,128)(2,1)S(1)}, bf16[16,384]{1,0:T(8,128)(2,1)S(1)}, u32[]{:S(2)}, u32[]{:S(2)}) collective-permute-start(bf16[16,384]{1,0:T(8,128)(2,1)S(1)} %get-tuple-element.100.refs_0_.token), channel_id=1, source_target_pairs={{0,6},{2,4},{4,2},{6,0},{1,7},{3,5},{5,3},{7,1},{8,14},{10,12},{12... | collective-permute-start | bytes 36872 | tf_op jit(solution)/shard_map/ppermute | solution.py:613
  21.3 0.6 collective-permute-start.4
  21.9 1.2 %shard_map.119 = (bf16[256,4352]{1,0:T(8,128)(2,1)S(1)}, bf16[256,768]{1,0:T(8,128)(2,1)S(1)}, bf16[256,768]{1,0:T(8,128)(2,1)S(1)}) custom-call(bf16[32,128,256]{2,1,0:T(8,128)(2,1)S(1)} %copy-done.1, bf16[1,128,256]{2,1,0:T(8,128)(2,1)S(1)} %get-tuple-element.96.top, bf16[1,128,256]{2,1,0:T(8,128)(2,1)S(1)} %get-tuple-element.97.bot, ...), custom_call_target="tpu_custom_call" | custom-call | flops 1207959552 | bytes 1048576 | tf_op jit(solution)/shard_map/pallas_call | solution.py:589
  23.1 2.7 %collective-permute-done.5.refs_2_ = bf16[16,384]{1,0:T(8,128)(2,1)S(1)} collective-permute-done((bf16[16,384]{1,0:T(8,128)(2,1)S(1)}, bf16[16,384]{1,0:T(8,128)(2,1)S(1)}, u32[]{:S(2)}, u32[]{:S(2)}) %collective-permute-start.5) | collective-permute-done | bytes 12320 | tf_op jit(solution)/shard_map/ppermute | solution.py:613
  25.9 1.2 %collective-permute-done.7.refs_1_ = bf16[4,16,384]{2,1,0:T(8,128)(2,1)S(1)} collective-permute-done((bf16[4,16,384]{2,1,0:T(8,128)(2,1)S(1)}, bf16[4,16,384]{2,1,0:T(8,128)(2,1)S(1)}, u32[]{:S(2)}, u32[]{:S(2)}) %collective-permute-start.7) | collective-permute-done | bytes 49184 | tf_op jit(solution)/shard_map/ppermute | solution.py:687
  27.2 2.3 %shard_map.120 = (f32[4,128,256]{2,1,0:T(8,128)S(1)}, bf16[16,128]{1,0:T(8,128)(2,1)S(1)}) custom-call(bf16[4,16,384]{2,1,0:T(8,128)(2,1)S(1)} %shard_map.118.refs_0_, bf16[4,16,384]{2,1,0:T(8,128)(2,1)S(1)} %collective-permute-done.7.refs_1_, f32[16,256]{1,0:T(8,128)S(1)} %get-tuple-element.103.refs_2_, bf16[256,768]{1,0:T(8,128)(2,1)S(1)} %get-tuple-element.104.refs_3_, ...), custom_call_target="tpu_custom_call" | custom-call | flops 1073741824 | bytes 1048576 | tf_op jit(solution)/shard_map/pallas_call | solution.py:589
  29.5 5.4 %shard_map.121 = (bf16[4096,768]{1,0:T(8,128)(2,1)S(1)}, bf16[2304,128]{1,0:T(8,128)(2,1)S(1)}, bf16[2304,128]{1,0:T(8,128)(2,1)S(1)}, bf16[1,128,256]{2,1,0:T(8...) custom-call(f32[4,128,256]{2,1,0:T(8,128)S(1)} %get-tuple-element.106.spr, ...), custom_call_target="tpu_custom_call" | custom-call | flops 4831838208 | bytes 1048576 | tf_op jit(solution)/shard_map/pallas_call | solution.py:589
  34.9 0.2 collective-permute-start.8
  35.1 4.2 %collective-permute-start.12 = (bf16[1,128,256]{2,1,0:T(8,128)(2,1)S(1)}, bf16[1,128,256]{2,1,0:T(8,128)(2,1)S(1)}, u32[]{:S(2)}, u32[]{:S(2)}) collective-permute-start(bf16[1,128,256]{2,1,0:T(8,128)(2,1)S(1)} %get-tuple-element.128), channel_id=1, source_target_pairs={{0,8},{16,24},{8,0},{24,16},{1,9},{17,25},{9,1},{25,17},{2,10},{18... | collective-permute-start | bytes 196616 | tf_op jit(solution)/shard_map/ppermute | solution.py:609
  39.3 0.9 %collective-permute-start.13 = (bf16[1,128,256]{2,1,0:T(8,128)(2,1)S(1)}, bf16[1,128,256]{2,1,0:T(8,128)(2,1)S(1)}, u32[]{:S(2)}, u32[]{:S(2)}) collective-permute-start(bf16[1,128,256]{2,1,0:T(8,128)(2,1)S(1)} %get-tuple-element.129), channel_id=1, source_target_pairs={{8,16},{16,8},{9,17},{17,9},{10,18},{18,10},{11,19},{19,11},{12,20... | collective-permute-start | bytes 196616 | tf_op jit(solution)/shard_map/ppermute | solution.py:609
  40.2 0.3 shard_map.122
  40.5 1.4 %collective-permute-start.9 = (bf16[592,128]{1,0:T(8,128)(2,1)S(1)}, bf16[592,128]{1,0:T(8,128)(2,1)S(1)}, u32[]{:S(2)}, u32[]{:S(2)}) collective-permute-start(bf16[592,128]{1,0:T(8,128)(2,1)S(1)} %get-tuple-element.121), channel_id=1, source_target_pairs={{0,24},{8,16},{16,8},{24,0},{1,25},{9,17},{17,9},{25,1},{2,26},{10... | collective-permute-start | bytes 454664 | tf_op jit(solution)/shard_map/ppermute | solution.py:613
  41.9 2.7 %collective-permute-start.10 = (bf16[592,128]{1,0:T(8,128)(2,1)S(1)}, bf16[592,128]{1,0:T(8,128)(2,1)S(1)}, u32[]{:S(2)}, u32[]{:S(2)}) collective-permute-start(bf16[592,128]{1,0:T(8,128)(2,1)S(1)} %get-tuple-element.122), channel_id=1, source_target_pairs={{0,16},{8,24},{16,0},{24,8},{1,17},{9,25},{17,1},{25,9},{2,18},{10... | collective-permute-start | bytes 454664 | tf_op jit(solution)/shard_map/ppermute | solution.py:613
  44.7 0.1 collective-permute-start.11
  44.8 1.7 %shard_map.123 = (bf16[10,128,256]{2,1,0:T(8,128)(2,1)S(1)}, f32[2,16,256]{2,1,0:T(8,128)S(1)}) custom-call(bf16[4096,768]{1,0:T(8,128)(2,1)S(1)} %get-tuple-element.151.wide, f32[4,128,256]{2,1,0:T(8,128)S(1)} %get-tuple-element.106.spread, bf16[9,256,256]{2,1,0:T(8,128)(2,1)S(1)} %copy-done), custom_call_target="tpu_custom_call" | custom-call | flops 1610612736 | bytes 1048576 | tf_op jit(solution)/shard_map/pallas_call | solution.py:589
  46.7 0.7 collective-permute-start.15
  47.3 0.9 %collective-permute-done.9.refs_1_ = bf16[592,128]{1,0:T(8,128)(2,1)S(1)} collective-permute-done((bf16[592,128]{1,0:T(8,128)(2,1)S(1)}, bf16[592,128]{1,0:T(8,128)(2,1)S(1)}, u32[]{:S(2)}, u32[]{:S(2)}) %collective-permute-start.9) | collective-permute-done | bytes 151584 | tf_op jit(solution)/shard_map/ppermute | solution.py:613
  48.2 2.7 %collective-permute-done.10.refs_2_ = bf16[592,128]{1,0:T(8,128)(2,1)S(1)} collective-permute-done((bf16[592,128]{1,0:T(8,128)(2,1)S(1)}, bf16[592,128]{1,0:T(8,128)(2,1)S(1)}, u32[]{:S(2)}, u32[]{:S(2)}) %collective-permute-start.10) | collective-permute-done | bytes 151584 | tf_op jit(solution)/shard_map/ppermute | solution.py:613
  50.9 1.1 %collective-permute-done.11.refs_3_ = bf16[592,128]{1,0:T(8,128)(2,1)S(1)} collective-permute-done((bf16[592,128]{1,0:T(8,128)(2,1)S(1)}, bf16[592,128]{1,0:T(8,128)(2,1)S(1)}, u32[]{:S(2)}, u32[]{:S(2)}) %collective-permute-start.11) | collective-permute-done | bytes 151584 | tf_op jit(solution)/shard_map/ppermute | solution.py:613
  52.0 0.7 shard_map.124
  52.7 1.4 %collective-permute-start.16 = (bf16[144,128]{1,0:T(8,128)(2,1)S(1)}, bf16[144,128]{1,0:T(8,128)(2,1)S(1)}, u32[]{:S(2)}, u32[]{:S(2)}) collective-permute-start(bf16[144,128]{1,0:T(8,128)(2,1)S(1)} %get-tuple-element.147), channel_id=1, source_target_pairs={{0,6},{2,4},{4,2},{6,0},{1,7},{3,5},{5,3},{7,1},{8,14},{10,12},{12... | collective-permute-start | bytes 110600 | tf_op jit(solution)/shard_map/ppermute | solution.py:613
  54.1 0.6 collective-permute-start.17
  54.7 2.4 %collective-permute-start.18 = (bf16[144,128]{1,0:T(8,128)(2,1)S(1)}, bf16[144,128]{1,0:T(8,128)(2,1)S(1)}, u32[]{:S(2)}, u32[]{:S(2)}) collective-permute-start(bf16[144,128]{1,0:T(8,128)(2,1)S(1)} %get-tuple-element.149), channel_id=1, source_target_pairs={{0,2},{2,0},{4,6},{6,4},{1,3},{3,1},{5,7},{7,5},{8,10},{10,8},{12,... | collective-permute-start | bytes 110600 | tf_op jit(solution)/shard_map/ppermute | solution.py:613
  57.0 1.6 %collective-permute-done.16.refs_1_ = bf16[144,128]{1,0:T(8,128)(2,1)S(1)} collective-permute-done((bf16[144,128]{1,0:T(8,128)(2,1)S(1)}, bf16[144,128]{1,0:T(8,128)(2,1)S(1)}, u32[]{:S(2)}, u32[]{:S(2)}) %collective-permute-start.16) | collective-permute-done | bytes 36896 | tf_op jit(solution)/shard_map/ppermute | solution.py:613
  58.6 0.4 collective-permute-done.17.refs_2_
  59.1 0.4 collective-permute-done.18.refs_3_
  59.4 2.4 %collective-permute-start.21 = (bf16[144,128]{1,0:T(8,128)(2,1)S(1)}, bf16[144,128]{1,0:T(8,128)(2,1)S(1)}, u32[]{:S(2)}, u32[]{:S(2)}) collective-permute-start(bf16[144,128]{1,0:T(8,128)(2,1)S(1)} %shard_map.126.refs_0_), channel_id=1, source_target_pairs={{0,6},{2,4},{4,2},{6,0},{1,7},{3,5},{5,3},{7,1},{8,14},{10,12},{12... | collective-permute-start | bytes 110600 | tf_op jit(solution)/shard_map/ppermute | solution.py:613
  61.8 0.7 collective-permute-start.20
  62.6 1.3 %collective-permute-start.19 = (bf16[144,128]{1,0:T(8,128)(2,1)S(1)}, bf16[144,128]{1,0:T(8,128)(2,1)S(1)}, u32[]{:S(2)}, u32[]{:S(2)}) collective-permute-start(bf16[144,128]{1,0:T(8,128)(2,1)S(1)} %shard_map.126.refs_0_), channel_id=1, source_target_pairs={{0,2},{2,0},{4,6},{6,4},{1,3},{3,1},{5,7},{7,5},{8,10},{10,8},{12,... | collective-permute-start | bytes 110600 | tf_op jit(solution)/shard_map/ppermute | solution.py:613
  63.9 1.7 %collective-permute-done.21.refs_3_ = bf16[144,128]{1,0:T(8,128)(2,1)S(1)} collective-permute-done((bf16[144,128]{1,0:T(8,128)(2,1)S(1)}, bf16[144,128]{1,0:T(8,128)(2,1)S(1)}, u32[]{:S(2)}, u32[]{:S(2)}) %collective-permute-start.21) | collective-permute-done | bytes 36896 | tf_op jit(solution)/shard_map/ppermute | solution.py:613
  65.6 1.2 %collective-permute-done.20.refs_2_ = bf16[144,128]{1,0:T(8,128)(2,1)S(1)} collective-permute-done((bf16[144,128]{1,0:T(8,128)(2,1)S(1)}, bf16[144,128]{1,0:T(8,128)(2,1)S(1)}, u32[]{:S(2)}, u32[]{:S(2)}) %collective-permute-start.20) | collective-permute-done | bytes 36896 | tf_op jit(solution)/shard_map/ppermute | solution.py:613
  66.8 0.1 collective-permute-done.19.refs_1_
  66.9 1.4 %collective-permute-start.24 = (bf16[4,144,128]{2,1,0:T(8,128)(2,1)S(1)}, bf16[4,144,128]{2,1,0:T(8,128)(2,1)S(1)}, u32[]{:S(2)}, u32[]{:S(2)}) collective-permute-start(bf16[4,144,128]{2,1,0:T(8,128)(2,1)S(1)} %shard_map.127.refs_0_), channel_id=1, source_target_pairs={{0,24},{8,16},{16,8},{24,0},{1,25},{9,17},{17,9},{25,1},{2,26},{10... | collective-permute-start | bytes 442376 | tf_op jit(solution)/shard_map/ppermute | solution.py:613
  68.3 1.5 %collective-permute-start.23 = (bf16[4,144,128]{2,1,0:T(8,128)(2,1)S(1)}, bf16[4,144,128]{2,1,0:T(8,128)(2,1)S(1)}, u32[]{:S(2)}, u32[]{:S(2)}) collective-permute-start(bf16[4,144,128]{2,1,0:T(8,128)(2,1)S(1)} %shard_map.127.refs_0_), channel_id=1, source_target_pairs={{0,16},{8,24},{16,0},{24,8},{1,17},{9,25},{17,1},{25,9},{2,18},{10... | collective-permute-start | bytes 442376 | tf_op jit(solution)/shard_map/ppermute | solution.py:613
  69.8 0.6 collective-permute-start.22
  70.5 4.7 %shard_map.128 = bf16[32,128,256]{2,1,0:T(8,128)(2,1)} custom-call(bf16[4096,768]{1,0:T(8,128)(2,1)S(1)} %get-tuple-element.151.wide, bf16[1,128,256]{2,1,0:T(8,128)(2,1)S(1)} %get-tuple-element.152.top, bf16[1,128,256]{2,1,0:T(8,128)(2,1)S(1)} %get-tuple-element.153.bot, bf16[48,256]{1,0:T(8,128)(2,1)S(1)} %collective-permute-done.14.even, ...), custom_call_target="tpu_custom_call" | custom-call | flops 2415919104 | bytes 1048576 | tf_op jit(solution)/shard_map/pallas_call | solution.py:589
  75.2 0.8 %collective-permute-done.22.refs_1_ = bf16[4,144,128]{2,1,0:T(8,128)(2,1)S(1)} collective-permute-done((bf16[4,144,128]{2,1,0:T(8,128)(2,1)S(1)}, bf16[4,144,128]{2,1,0:T(8,128)(2,1)S(1)}, u32[]{:S(2)}, u32[]{:S(2)}) %collective-permute-start.22) | collective-permute-done | bytes 147488 | tf_op jit(solution)/shard_map/ppermute | solution.py:613
  76.1 1.1 %shard_map.130.refs_1_ = f32[2304,256]{1,0:T(8,128)} custom-call(bf16[4,4,144,128]{3,2,1,0:T(8,128)(2,1)S(1)} %shard_map.129.refs_0_), custom_call_target="tpu_custom_call" | custom-call | flops 1048576 | bytes 1048576 | tf_op jit(solution)/shard_map/pallas_call | solution.py:589
  77.2 0.9 %collective-permute-done.25.refs_0_ = bf16[4,4,144,128]{3,2,1,0:T(8,128)(2,1)S(1)} collective-permute-done((bf16[4,4,144,128]{3,2,1,0:T(8,128)(2,1)S(1)}, bf16[4,4,144,128]{3,2,1,0:T(8,128)(2,1)S(1)}, u32[]{:S(2)}, u32[]{:S(2)}) %collective-permute-start.25) | collective-permute-done | bytes 589856 | tf_op jit(solution)/shard_map/ppermute | solution.py:773
  78.1 1.1 %shard_map.131 = f32[2304,256]{1,0:T(8,128)} custom-call(bf16[4,4,144,128]{3,2,1,0:T(8,128)(2,1)S(1)} %collective-permute-done.25.refs_0_, f32[2304,256]{1,0:T(8,128)} %shard_map.130.refs_1_), custom_call_target="tpu_custom_call", output_to_operand_aliasing={{}: (1, {})} | custom-call | flops 1048576 | bytes 1048576 | tf_op jit(solution)/shard_map/pallas_call | solution.py:589
  (43 shorter events, 0.6 us)
Async XLA Ops:
  1.5 3.7 %copy-start = (bf16[9,256,256]{2,1,0:T(8,128)(2,1)S(1)}, bf16[9,256,256]{2,1,0:T(8,128)(2,1)}, u32[]{:S(2)}) copy-start(bf16[9,256,256]{2,1,0:T(8,128)(2,1)} %weight.5) | copy-start | bytes 3538948
  1.5 3.7 %copy-start.1 = (bf16[32,128,256]{2,1,0:T(8,128)(2,1)S(1)}, bf16[32,128,256]{2,1,0:T(8,128)(2,1)}, u32[]{:S(2)}) copy-start(bf16[32,128,256]{2,1,0:T(8,128)(2,1)} %feat.3) | copy-start | bytes 6291460
  1.5 3.7 %copy-start.3 = (s32[2,8]{1,0:T(2,128)S(1)}, s32[2,8]{1,0:T(2,128)}, u32[]{:S(2)}) copy-start(s32[2,8]{1,0:T(2,128)} %flags_ref.1) | copy-start | bytes 196
  1.6 7.4 %collective-permute-start = (bf16[1,128,256]{2,1,0:T(8,128)(2,1)S(1)}, bf16[1,128,256]{2,1,0:T(8,128)(2,1)S(1)}, u32[]{:S(2)}, u32[]{:S(2)}) collective-permute-start(bf16[1,128,256]{2,1,0:T(8,128)(2,1)S(1)} %get-tuple-element.86), channel_id=1, source_target_pairs={{0,8},{16,24},{8,0},{24,16},{1,9},{17,25},{9,1},{25,17},{2,10},{18... | collective-permute-start | bytes 196616 | tf_op jit(solution)/shard_map/ppermute | solution.py:609
  4.6 4.4 %collective-permute-start.1 = (bf16[1,128,256]{2,1,0:T(8,128)(2,1)S(1)}, bf16[1,128,256]{2,1,0:T(8,128)(2,1)S(1)}, u32[]{:S(2)}, u32[]{:S(2)}) collective-permute-start(bf16[1,128,256]{2,1,0:T(8,128)(2,1)S(1)} %get-tuple-element.87), channel_id=1, source_target_pairs={{8,16},{16,8},{9,17},{17,9},{10,18},{18,10},{11,19},{19,11},{12,20... | collective-permute-start | bytes 196616 | tf_op jit(solution)/shard_map/ppermute | solution.py:609
  9.1 4.6 %collective-permute-start.2 = (bf16[48,256]{1,0:T(8,128)(2,1)S(1)}, bf16[48,256]{1,0:T(8,128)(2,1)S(1)}, u32[]{:S(2)}, u32[]{:S(2)}) collective-permute-start(bf16[48,256]{1,0:T(8,128)(2,1)S(1)} %get-tuple-element.98), channel_id=1, source_target_pairs={{0,1},{2,3},{4,5},{6,7},{1,0},{3,2},{5,4},{7,6},{8,9},{10,11},{12,... | collective-permute-start | bytes 73736 | tf_op jit(solution)/shard_map/ppermute | solution.py:609
  9.2 4.6 %copy-start.2 = (bf16[4,256,256]{2,1,0:T(8,128)(2,1)S(1)}, bf16[4,256,256]{2,1,0:T(8,128)(2,1)}, u32[]{:S(2)}) copy-start(bf16[4,256,256]{2,1,0:T(8,128)(2,1)} %refs_6_.1) | copy-start | bytes 1572868
  9.2 4.6 %copy-start.4 = (s32[1,1,16,1]{2,3,1,0:T(1,128)S(1)}, s32[1,1,16,1]{2,3,1,0:T(1,128)}, u32[]{:S(2)}) copy-start(s32[1,1,16,1]{2,3,1,0:T(1,128)} %param.11) | copy-start | bytes 196
  9.2 4.5 %collective-permute-start.3 = (bf16[48,256]{1,0:T(8,128)(2,1)S(1)}, bf16[48,256]{1,0:T(8,128)(2,1)S(1)}, u32[]{:S(2)}, u32[]{:S(2)}) collective-permute-start(bf16[48,256]{1,0:T(8,128)(2,1)S(1)} %get-tuple-element.99), channel_id=1, source_target_pairs={{1,2},{3,4},{5,6},{2,1},{4,3},{6,5},{9,10},{11,12},{13,14},{10,9},... | collective-permute-start | bytes 73736 | tf_op jit(solution)/shard_map/ppermute | solution.py:609
  13.7 8.1 %copy-start.5 = (f32[256,256]{1,0:T(8,128)S(1)}, f32[256,256]{1,0:T(8,128)}, u32[]{:S(2)}) copy-start(f32[256,256]{1,0:T(8,128)} %w_query.1) | copy-start | bytes 786436
  13.8 8.1 %copy-start.6 = (f32[256,256]{1,0:T(8,128)S(1)}, f32[256,256]{1,0:T(8,128)}, u32[]{:S(2)}) copy-start(f32[256,256]{1,0:T(8,128)} %w_key.1) | copy-start | bytes 786436
  13.8 8.1 %copy-start.7 = (f32[256,256]{1,0:T(8,128)S(1)}, f32[256,256]{1,0:T(8,128)}, u32[]{:S(2)}) copy-start(f32[256,256]{1,0:T(8,128)} %w_value.1) | copy-start | bytes 786436
  15.8 11.4 %copy-start.8 = (f32[256]{0:T(256)S(1)}, f32[256]{0:T(256)}, u32[]{:S(2)}) copy-start(f32[256]{0:T(256)} %param.17) | copy-start | bytes 3076
  15.8 7.3 %collective-permute-start.6 = (bf16[16,384]{1,0:T(8,128)(2,1)S(1)}, bf16[16,384]{1,0:T(8,128)(2,1)S(1)}, u32[]{:S(2)}, u32[]{:S(2)}) collective-permute-start(bf16[16,384]{1,0:T(8,128)(2,1)S(1)} %get-tuple-element.100.refs_0_.token), channel_id=1, source_target_pairs={{0,6},{2,4},{4,2},{6,0},{1,7},{3,5},{5,3},{7,1},{8,14},{10,12},{12... | collective-permute-start | bytes 36872 | tf_op jit(solution)/shard_map/ppermute | solution.py:613
  21.2 4.6 %collective-permute-start.5 = (bf16[16,384]{1,0:T(8,128)(2,1)S(1)}, bf16[16,384]{1,0:T(8,128)(2,1)S(1)}, u32[]{:S(2)}, u32[]{:S(2)}) collective-permute-start(bf16[16,384]{1,0:T(8,128)(2,1)S(1)} %get-tuple-element.100.refs_0_.token), channel_id=1, source_target_pairs={{0,4},{2,6},{4,0},{6,2},{1,5},{3,7},{5,1},{7,3},{8,12},{10,14},{12... | collective-permute-start | bytes 36872 | tf_op jit(solution)/shard_map/ppermute | solution.py:613
  21.3 4.6 %collective-permute-start.4 = (bf16[16,384]{1,0:T(8,128)(2,1)S(1)}, bf16[16,384]{1,0:T(8,128)(2,1)S(1)}, u32[]{:S(2)}, u32[]{:S(2)}) collective-permute-start(bf16[16,384]{1,0:T(8,128)(2,1)S(1)} %get-tuple-element.100.refs_0_.token), channel_id=1, source_target_pairs={{0,2},{2,0},{4,6},{6,4},{1,3},{3,1},{5,7},{7,5},{8,10},{10,8},{12,... | collective-permute-start | bytes 36872 | tf_op jit(solution)/shard_map/ppermute | solution.py:613
  25.9 1.3 %collective-permute-start.7 = (bf16[4,16,384]{2,1,0:T(8,128)(2,1)S(1)}, bf16[4,16,384]{2,1,0:T(8,128)(2,1)S(1)}, u32[]{:S(2)}, u32[]{:S(2)}) collective-permute-start(bf16[4,16,384]{2,1,0:T(8,128)(2,1)S(1)} %shard_map.118.refs_0_), channel_id=1, source_target_pairs={{0,1},{1,0},{2,3},{3,2},{4,5},{5,4},{6,7},{7,6},{8,9},{9,8},{10,11... | collective-permute-start | bytes 147464 | tf_op jit(solution)/shard_map/ppermute | solution.py:687
  34.9 5.3 %collective-permute-start.8 = (bf16[2304,128]{1,0:T(8,128)(2,1)S(1)}, bf16[2304,128]{1,0:T(8,128)(2,1)S(1)}, u32[]{:S(2)}, u32[]{:S(2)}) collective-permute-start(bf16[2304,128]{1,0:T(8,128)(2,1)S(1)} %get-tuple-element.113), channel_id=1, source_target_pairs={{0,1},{1,0},{2,3},{3,2},{4,5},{5,4},{6,7},{7,6},{8,9},{9,8},{10,11... | collective-permute-start | bytes 1769480 | tf_op jit(solution)/shard_map/ppermute | solution.py:713
  35.1 11.4 %collective-permute-start.12 = (bf16[1,128,256]{2,1,0:T(8,128)(2,1)S(1)}, bf16[1,128,256]{2,1,0:T(8,128)(2,1)S(1)}, u32[]{:S(2)}, u32[]{:S(2)}) collective-permute-start(bf16[1,128,256]{2,1,0:T(8,128)(2,1)S(1)} %get-tuple-element.128), channel_id=1, source_target_pairs={{0,8},{16,24},{8,0},{24,16},{1,9},{17,25},{9,1},{25,17},{2,10},{18... | collective-permute-start | bytes 196616 | tf_op jit(solution)/shard_map/ppermute | solution.py:609
  39.3 7.2 %collective-permute-start.13 = (bf16[1,128,256]{2,1,0:T(8,128)(2,1)S(1)}, bf16[1,128,256]{2,1,0:T(8,128)(2,1)S(1)}, u32[]{:S(2)}, u32[]{:S(2)}) collective-permute-start(bf16[1,128,256]{2,1,0:T(8,128)(2,1)S(1)} %get-tuple-element.129), channel_id=1, source_target_pairs={{8,16},{16,8},{9,17},{17,9},{10,18},{18,10},{11,19},{19,11},{12,20... | collective-permute-start | bytes 196616 | tf_op jit(solution)/shard_map/ppermute | solution.py:609
  40.5 7.6 %collective-permute-start.9 = (bf16[592,128]{1,0:T(8,128)(2,1)S(1)}, bf16[592,128]{1,0:T(8,128)(2,1)S(1)}, u32[]{:S(2)}, u32[]{:S(2)}) collective-permute-start(bf16[592,128]{1,0:T(8,128)(2,1)S(1)} %get-tuple-element.121), channel_id=1, source_target_pairs={{0,24},{8,16},{16,8},{24,0},{1,25},{9,17},{17,9},{25,1},{2,26},{10... | collective-permute-start | bytes 454664 | tf_op jit(solution)/shard_map/ppermute | solution.py:613
  41.9 9.0 %collective-permute-start.10 = (bf16[592,128]{1,0:T(8,128)(2,1)S(1)}, bf16[592,128]{1,0:T(8,128)(2,1)S(1)}, u32[]{:S(2)}, u32[]{:S(2)}) collective-permute-start(bf16[592,128]{1,0:T(8,128)(2,1)S(1)} %get-tuple-element.122), channel_id=1, source_target_pairs={{0,16},{8,24},{16,0},{24,8},{1,17},{9,25},{17,1},{25,9},{2,18},{10... | collective-permute-start | bytes 454664 | tf_op jit(solution)/shard_map/ppermute | solution.py:613
  44.7 7.3 %collective-permute-start.11 = (bf16[592,128]{1,0:T(8,128)(2,1)S(1)}, bf16[592,128]{1,0:T(8,128)(2,1)S(1)}, u32[]{:S(2)}, u32[]{:S(2)}) collective-permute-start(bf16[592,128]{1,0:T(8,128)(2,1)S(1)} %get-tuple-element.123), channel_id=1, source_target_pairs={{0,8},{8,0},{16,24},{24,16},{1,9},{9,1},{17,25},{25,17},{2,10},{10... | collective-permute-start | bytes 454664 | tf_op jit(solution)/shard_map/ppermute | solution.py:613
  46.6 6.1 %collective-permute-start.14 = (bf16[48,256]{1,0:T(8,128)(2,1)S(1)}, bf16[48,256]{1,0:T(8,128)(2,1)S(1)}, u32[]{:S(2)}, u32[]{:S(2)}) collective-permute-start(bf16[48,256]{1,0:T(8,128)(2,1)S(1)} %get-tuple-element.144), channel_id=1, source_target_pairs={{0,1},{2,3},{4,5},{6,7},{1,0},{3,2},{5,4},{7,6},{8,9},{10,11},{12,... | collective-permute-start | bytes 73736 | tf_op jit(solution)/shard_map/ppermute | solution.py:609
  46.7 6.0 %collective-permute-start.15 = (bf16[48,256]{1,0:T(8,128)(2,1)S(1)}, bf16[48,256]{1,0:T(8,128)(2,1)S(1)}, u32[]{:S(2)}, u32[]{:S(2)}) collective-permute-start(bf16[48,256]{1,0:T(8,128)(2,1)S(1)} %get-tuple-element.145), channel_id=1, source_target_pairs={{1,2},{3,4},{5,6},{2,1},{4,3},{6,5},{9,10},{11,12},{13,14},{10,9},... | collective-permute-start | bytes 73736 | tf_op jit(solution)/shard_map/ppermute | solution.py:609
  52.7 6.0 %collective-permute-start.16 = (bf16[144,128]{1,0:T(8,128)(2,1)S(1)}, bf16[144,128]{1,0:T(8,128)(2,1)S(1)}, u32[]{:S(2)}, u32[]{:S(2)}) collective-permute-start(bf16[144,128]{1,0:T(8,128)(2,1)S(1)} %get-tuple-element.147), channel_id=1, source_target_pairs={{0,6},{2,4},{4,2},{6,0},{1,7},{3,5},{5,3},{7,1},{8,14},{10,12},{12... | collective-permute-start | bytes 110600 | tf_op jit(solution)/shard_map/ppermute | solution.py:613
  54.1 5.0 %collective-permute-start.17 = (bf16[144,128]{1,0:T(8,128)(2,1)S(1)}, bf16[144,128]{1,0:T(8,128)(2,1)S(1)}, u32[]{:S(2)}, u32[]{:S(2)}) collective-permute-start(bf16[144,128]{1,0:T(8,128)(2,1)S(1)} %get-tuple-element.148), channel_id=1, source_target_pairs={{0,4},{2,6},{4,0},{6,2},{1,5},{3,7},{5,1},{7,3},{8,12},{10,14},{12... | collective-permute-start | bytes 110600 | tf_op jit(solution)/shard_map/ppermute | solution.py:613
  54.7 4.7 %collective-permute-start.18 = (bf16[144,128]{1,0:T(8,128)(2,1)S(1)}, bf16[144,128]{1,0:T(8,128)(2,1)S(1)}, u32[]{:S(2)}, u32[]{:S(2)}) collective-permute-start(bf16[144,128]{1,0:T(8,128)(2,1)S(1)} %get-tuple-element.149), channel_id=1, source_target_pairs={{0,2},{2,0},{4,6},{6,4},{1,3},{3,1},{5,7},{7,5},{8,10},{10,8},{12,... | collective-permute-start | bytes 110600 | tf_op jit(solution)/shard_map/ppermute | solution.py:613
  59.4 6.1 %collective-permute-start.21 = (bf16[144,128]{1,0:T(8,128)(2,1)S(1)}, bf16[144,128]{1,0:T(8,128)(2,1)S(1)}, u32[]{:S(2)}, u32[]{:S(2)}) collective-permute-start(bf16[144,128]{1,0:T(8,128)(2,1)S(1)} %shard_map.126.refs_0_), channel_id=1, source_target_pairs={{0,6},{2,4},{4,2},{6,0},{1,7},{3,5},{5,3},{7,1},{8,14},{10,12},{12... | collective-permute-start | bytes 110600 | tf_op jit(solution)/shard_map/ppermute | solution.py:613
  61.8 5.0 %collective-permute-start.20 = (bf16[144,128]{1,0:T(8,128)(2,1)S(1)}, bf16[144,128]{1,0:T(8,128)(2,1)S(1)}, u32[]{:S(2)}, u32[]{:S(2)}) collective-permute-start(bf16[144,128]{1,0:T(8,128)(2,1)S(1)} %shard_map.126.refs_0_), channel_id=1, source_target_pairs={{0,4},{2,6},{4,0},{6,2},{1,5},{3,7},{5,1},{7,3},{8,12},{10,14},{12... | collective-permute-start | bytes 110600 | tf_op jit(solution)/shard_map/ppermute | solution.py:613
  62.6 4.4 %collective-permute-start.19 = (bf16[144,128]{1,0:T(8,128)(2,1)S(1)}, bf16[144,128]{1,0:T(8,128)(2,1)S(1)}, u32[]{:S(2)}, u32[]{:S(2)}) collective-permute-start(bf16[144,128]{1,0:T(8,128)(2,1)S(1)} %shard_map.126.refs_0_), channel_id=1, source_target_pairs={{0,2},{2,0},{4,6},{6,4},{1,3},{3,1},{5,7},{7,5},{8,10},{10,8},{12,... | collective-permute-start | bytes 110600 | tf_op jit(solution)/shard_map/ppermute | solution.py:613
  66.9 8.2 %collective-permute-start.24 = (bf16[4,144,128]{2,1,0:T(8,128)(2,1)S(1)}, bf16[4,144,128]{2,1,0:T(8,128)(2,1)S(1)}, u32[]{:S(2)}, u32[]{:S(2)}) collective-permute-start(bf16[4,144,128]{2,1,0:T(8,128)(2,1)S(1)} %shard_map.127.refs_0_), channel_id=1, source_target_pairs={{0,24},{8,16},{16,8},{24,0},{1,25},{9,17},{17,9},{25,1},{2,26},{10... | collective-permute-start | bytes 442376 | tf_op jit(solution)/shard_map/ppermute | solution.py:613
  68.3 6.8 %collective-permute-start.23 = (bf16[4,144,128]{2,1,0:T(8,128)(2,1)S(1)}, bf16[4,144,128]{2,1,0:T(8,128)(2,1)S(1)}, u32[]{:S(2)}, u32[]{:S(2)}) collective-permute-start(bf16[4,144,128]{2,1,0:T(8,128)(2,1)S(1)} %shard_map.127.refs_0_), channel_id=1, source_target_pairs={{0,16},{8,24},{16,0},{24,8},{1,17},{9,25},{17,1},{25,9},{2,18},{10... | collective-permute-start | bytes 442376 | tf_op jit(solution)/shard_map/ppermute | solution.py:613
  69.8 6.1 %collective-permute-start.22 = (bf16[4,144,128]{2,1,0:T(8,128)(2,1)S(1)}, bf16[4,144,128]{2,1,0:T(8,128)(2,1)S(1)}, u32[]{:S(2)}, u32[]{:S(2)}) collective-permute-start(bf16[4,144,128]{2,1,0:T(8,128)(2,1)S(1)} %shard_map.127.refs_0_), channel_id=1, source_target_pairs={{0,8},{8,0},{16,24},{24,16},{1,9},{9,1},{17,25},{25,17},{2,10},{10... | collective-permute-start | bytes 442376 | tf_op jit(solution)/shard_map/ppermute | solution.py:613
  76.0 2.1 %collective-permute-start.25 = (bf16[4,4,144,128]{3,2,1,0:T(8,128)(2,1)S(1)}, bf16[4,4,144,128]{3,2,1,0:T(8,128)(2,1)S(1)}, u32[]{:S(2)}, u32[]{:S(2)}) collective-permute-start(bf16[4,4,144,128]{3,2,1,0:T(8,128)(2,1)S(1)} %shard_map.129.refs_0_), channel_id=1, source_target_pairs={{0,1},{1,0},{2,3},{3,2},{4,5},{5,4},{6,7},{7,6},{8,9},{9,8},{10,11... | collective-permute-start | bytes 1769480 | tf_op jit(solution)/shard_map/ppermute | solution.py:773
where the time goes:
time: 79.6 us; the launch traced here: 79.4 us
  starting transfers between devices  33.6 us (42%)
  Pallas kernels  27.9 us (35%)
  waiting for transfers between devices  15.7 us (20%)
  between operations  1.2 us (2%)
  local copies, waits for them, and re-layouts  0.95 us (1%)
    pallas_call x20, Pallas kernels, run(): pl.pallas_call(body, in_specs=specs, out_shape=outs, scratch_shapes=list(...  27.9 us
    ppermute x15, starting transfers between devices, others(): lax.ppermute(values[k - 1], axis, [(i, i ^ k) for i in range(count)])  22.7 us
    ppermute x15, waiting for transfers between devices, others(): lax.ppermute(values[k - 1], axis, [(i, i ^ k) for i in range(count)])  13.6 us
    ppermute x8, starting transfers between devices, pairs(): lax.ppermute(value, axis, [(i, i + 1) for i in low] + [(i + 1, i) for i i...  10.5 us
  transfers between devices with their start and end apart: 26, of which 13 were waited for; matrix products, arithmetic and copies ran while one was open for 0% of the time, Pallas kernels for 21%

commit v1 on v0

--- a/solution.py
+++ b/solution.py
@@ -281,18 +281,22 @@
         low_ref[:, i * CH : (i + 1) * CH] = low
 
 
-def attention_body(
-    mine, other, pooled_ref, high_w, low_w, cot, strided, spread_ref, emb_ref, band, grad_ref, *, seed_scale
-):
+def pair_body(one, two, out_ref):
+    out_ref[0:16] = one[...]
+    out_ref[16:32] = two[...]
+
+
+def attention_body(*refs, seed_scale):
+    *got, pooled_ref, high_w, low_w, cot, strided, spread_ref, emb_ref, band, grad_ref = refs
     gz, core = lax.axis_index("gz"), lax.axis_index("core")
 
     def rows_of(depth, other):
         return pl.ds(pl.multiple_of(depth * 32 + other * 16, 16), 16)
 
-    for k in range(mine.shape[0]):
+    for k, piece in enumerate(got):
         depth = lax.bitwise_xor(gz, k)
-        band[rows_of(depth, core)] = mine[k]
-        band[rows_of(depth, 1 - core)] = other[k]
+        band[rows_of(depth, core)] = piece[0:16]
+        band[rows_of(depth, 1 - core)] = piece[16:32]
     count = band.shape[0]
     tokens, group = band[:, 0:CH], band[:, CH:]
     pair = nt(group, group)
@@ -353,7 +357,7 @@
             spread_ref[band * 2 + a] = spread[:, a * CH : (a + 1) * CH]
 
 
-GROUPS = (4, 12, 16)
+GROUPS = (6, 10, 16)
 
 
 def weight_body(
@@ -672,6 +676,10 @@
     def stacked(terms):
         return run(stack_body, terms, shape((len(terms),) + terms[0].shape, BF16), mib=4)
 
+    both = run(
+        pair_body, (token, lax.ppermute(token, "core", swap)), shape((32, CH + LANES), BF16), mib=1
+    )
+    pieces = [both] + others([both] * (gz_count - 1), "gz", gz_count)
     turned, high_w, low_w = run(
         turn_body,
         (features, top, bot, w_query, w_key, w_value, token),
@@ -679,12 +687,10 @@
         flops=conv_flops // 4,
         mib=12,
     )
-    tokens = stacked([token] + others([token] * (gz_count - 1), "gz", gz_count))
-    tokens, high_w = lax.optimization_barrier((tokens, high_w))
     count = 16 * gx_count
     spread, emb = run(
         lambda *refs: attention_body(*refs, seed_scale=loss_scale * norm_scale),
-        (tokens, lax.ppermute(tokens, "core", swap), pooled, high_w, low_w, cotangent.reshape(1, CH), w_stride),
+        (*pieces, pooled, high_w, low_w, cotangent.reshape(1, CH), w_stride),
         [shape((4, COLS, CH), F32), shape((16, LANES), BF16)],
         [pltpu.VMEM((count, CH + LANES), BF16), pltpu.VMEM((count, 3 * CH), F32)],
         flops=1 << 30,

time: 79.6 us -> 78.9 us (level)
  waiting for transfers between devices: 15.7 us -> 13.9 us
  starting transfers between devices: 33.6 us -> 34.8 us
    ppermute x1, starting transfers between devices: 0.07 us -> 2.98 us  [per_device(): lax.ppermute(token, 'core', swap)]
    ppermute x15, starting transfers between devices: 22.7 us -> 21 us  [others(): lax.ppermute(values[k - 1], axis, [(i, i ^ k) for i in range(count)])]
    ppermute x15, waiting for transfers between devices: 13.6 us -> 12.2 us  [others(): lax.ppermute(values[k - 1], axis, [(i, i ^ k) for i in range(count)])]
  transfers between devices with their start and end apart: 26 -> 26, of which waited for: 13 -> 12; matrix products, arithmetic and copies ran while one was open for 0% -> 0% of each run, Pallas kernels for 21% -> 22%
where the time goes in v1:
time: 78.9 us; the launch traced here: 78.7 us
  starting transfers between devices  34.8 us (44%)
  Pallas kernels  27.9 us (35%)
  waiting for transfers between devices  13.9 us (18%)
  between operations  1.18 us (1%)
  local copies, waits for them, and re-layouts  0.94 us (1%)
    pallas_call x20, Pallas kernels, run(): pl.pallas_call(body, in_specs=specs, out_shape=outs, scratch_shapes=list(...  27.9 us
    ppermute x15, starting transfers between devices, others(): lax.ppermute(values[k - 1], axis, [(i, i ^ k) for i in range(count)])  21 us
    ppermute x15, waiting for transfers between devices, others(): lax.ppermute(values[k - 1], axis, [(i, i ^ k) for i in range(count)])  12.2 us
    ppermute x8, starting transfers between devices, pairs(): lax.ppermute(value, axis, [(i, i + 1) for i in low] + [(i + 1, i) for i i...  10.6 us
    ppermute x1, starting transfers between devices, per_device(): lax.ppermute(token, 'core', swap)  2.98 us
  transfers between devices with their start and end apart: 26, of which 12 were waited for; matrix products, arithmetic and copies ran while one was open for 0% of the time, Pallas kernels for 22%

profile of v1, /device:TPU:0, one launch (start us, length us, event | category | flops | bytes accessed | tf_op | source)
XLA Modules:
  0.0 78.7 jit_solution(2987142795457630289)
XLA Ops:
  0.6 0.9 %fusion = (bf16[1,128,256]{2,1,0:T(8,128)(2,1)S(1)}, bf16[1,128,256]{2,1,0:T(8,128)(2,1)S(1)}) fusion(bf16[32,128,256]{2,1,0:T(8,128)(2,1)} %feat.3), kind=kLoop, calls=%fused_computation | loop fusion | bytes 262144 | tf_op jit(solution)/shard_map/slice | solution.py:650
  1.6 3.0 %collective-permute-start = (bf16[1,128,256]{2,1,0:T(8,128)(2,1)S(1)}, bf16[1,128,256]{2,1,0:T(8,128)(2,1)S(1)}, u32[]{:S(2)}, u32[]{:S(2)}) collective-permute-start(bf16[1,128,256]{2,1,0:T(8,128)(2,1)S(1)} %get-tuple-element.84), channel_id=1, source_target_pairs={{0,8},{16,24},{8,0},{24,16},{1,9},{17,25},{9,1},{25,17},{2,10},{18... | collective-permute-start | bytes 196616 | tf_op jit(solution)/shard_map/ppermute | solution.py:613
  4.6 0.7 collective-permute-start.1
  5.3 3.5 %shard_map.112 = (bf16[16,128,256]{2,1,0:T(8,128)(2,1)S(1)}, f32[2,128,256]{2,1,0:T(8,128)S(1)}, f32[6,16,256]{2,1,0:T(8,128)S(1)}) custom-call(s32[2,8]{1,0:T(2,128)S(1)} %copy-done.3, bf16[32,128,256]{2,1,0:T(8,128)(2,1)S(1)} %copy-done.1, bf16[9,256,256]{2,1,0:T(8,128)(2,1)S(1)} %copy-done), custom_call_target="tpu_custom_call" | custom-call | flops 2415919104 | bytes 1048576 | tf_op jit(solution)/shard_map/pallas_call | solution.py:593
  8.8 0.2 shard_map.113
  9.1 0.1 collective-permute-start.2
  9.2 1.0 %collective-permute-start.3 = (bf16[48,256]{1,0:T(8,128)(2,1)S(1)}, bf16[48,256]{1,0:T(8,128)(2,1)S(1)}, u32[]{:S(2)}, u32[]{:S(2)}) collective-permute-start(bf16[48,256]{1,0:T(8,128)(2,1)S(1)} %get-tuple-element.97), channel_id=1, source_target_pairs={{1,2},{3,4},{5,6},{2,1},{4,3},{6,5},{9,10},{11,12},{13,14},{10,9},... | collective-permute-start | bytes 73736 | tf_op jit(solution)/shard_map/ppermute | solution.py:613
  10.2 3.5 %shard_map.116 = (bf16[16,128,256]{2,1,0:T(8,128)(2,1)S(1)}, f32[2,128,256]{2,1,0:T(8,128)S(1)}, f32[6,16,256]{2,1,0:T(8,128)S(1)}) custom-call(s32[2,8]{1,0:T(2,128)S(1)} %copy-done.3, bf16[32,128,256]{2,1,0:T(8,128)(2,1)S(1)} %copy-done.1, bf16[9,256,256]{2,1,0:T(8,128)(2,1)S(1)} %copy-done), custom_call_target="tpu_custom_call" | custom-call | flops 2415919104 | bytes 1048576 | tf_op jit(solution)/shard_map/pallas_call | solution.py:593
  13.8 2.0 %shard_map.117 = (f32[16,256]{1,0:T(8,128)S(1)}, bf16[16,384]{1,0:T(8,128)(2,1)S(1)}, bf16[2,128,256]{2,1,0:T(8,128)(2,1)S(1)}, f32[2,32,256]{2,1,0:T(8,128)S(1)}) custom-call(s32[2,8]{1,0:T(2,128)S(1)} %copy-done.3, bf16[32,128,256]{2,1,0:T(8,128)(2,1)S(1)} %copy-done.1, bf16[9,256,256]{2,1,0:T(8,128)(2,1)S(1)} %copy-done, ...), custom_call_target="tpu_custom_call" | custom-call | flops 603979776 | bytes 1048576 | tf_op jit(solution)/shard_map/pallas_call | solution.py:593
  15.8 3.0 %collective-permute-start.4 = (bf16[16,384]{1,0:T(8,128)(2,1)S(1)}, bf16[16,384]{1,0:T(8,128)(2,1)S(1)}, u32[]{:S(2)}, u32[]{:S(2)}) collective-permute-start(bf16[16,384]{1,0:T(8,128)(2,1)S(1)} %get-tuple-element.98.one.token), channel_id=1, source_target_pairs={{0,1},{1,0},{2,3},{3,2},{4,5},{5,4},{6,7},{7,6},{8,9},{9,8},{10,11... | collective-permute-start | bytes 36872 | tf_op jit(solution)/shard_map/ppermute | solution.py:680
  18.8 0.8 %collective-permute-done.4.two = bf16[16,384]{1,0:T(8,128)(2,1)S(1)} collective-permute-done((bf16[16,384]{1,0:T(8,128)(2,1)S(1)}, bf16[16,384]{1,0:T(8,128)(2,1)S(1)}, u32[]{:S(2)}, u32[]{:S(2)}) %collective-permute-start.4) | collective-permute-done | bytes 12320 | tf_op jit(solution)/shard_map/ppermute | solution.py:680
  19.6 2.8 %collective-permute-start.7 = (bf16[32,384]{1,0:T(8,128)(2,1)S(1)}, bf16[32,384]{1,0:T(8,128)(2,1)S(1)}, u32[]{:S(2)}, u32[]{:S(2)}) collective-permute-start(bf16[32,384]{1,0:T(8,128)(2,1)S(1)} %shard_map.118.refs_0_), channel_id=1, source_target_pairs={{0,6},{2,4},{4,2},{6,0},{1,7},{3,5},{5,3},{7,1},{8,14},{10,12},{12... | collective-permute-start | bytes 73736 | tf_op jit(solution)/shard_map/ppermute | solution.py:617
  22.4 0.3 collective-permute-start.6
  22.6 1.3 %collective-permute-start.5 = (bf16[32,384]{1,0:T(8,128)(2,1)S(1)}, bf16[32,384]{1,0:T(8,128)(2,1)S(1)}, u32[]{:S(2)}, u32[]{:S(2)}) collective-permute-start(bf16[32,384]{1,0:T(8,128)(2,1)S(1)} %shard_map.118.refs_0_), channel_id=1, source_target_pairs={{0,2},{2,0},{4,6},{6,4},{1,3},{3,1},{5,7},{7,5},{8,10},{10,8},{12,... | collective-permute-start | bytes 73736 | tf_op jit(solution)/shard_map/ppermute | solution.py:617
  24.0 1.2 %shard_map.119 = (bf16[256,4352]{1,0:T(8,128)(2,1)S(1)}, bf16[256,768]{1,0:T(8,128)(2,1)S(1)}, bf16[256,768]{1,0:T(8,128)(2,1)S(1)}) custom-call(bf16[32,128,256]{2,1,0:T(8,128)(2,1)S(1)} %copy-done.1, bf16[1,128,256]{2,1,0:T(8,128)(2,1)S(1)} %get-tuple-element.94.top, bf16[1,128,256]{2,1,0:T(8,128)(2,1)S(1)} %get-tuple-element.95.bot, ...), custom_call_target="tpu_custom_call" | custom-call | flops 1207959552 | bytes 1048576 | tf_op jit(solution)/shard_map/pallas_call | solution.py:593
  25.2 2.0 %collective-permute-done.6.refs_2_ = bf16[32,384]{1,0:T(8,128)(2,1)S(1)} collective-permute-done((bf16[32,384]{1,0:T(8,128)(2,1)S(1)}, bf16[32,384]{1,0:T(8,128)(2,1)S(1)}, u32[]{:S(2)}, u32[]{:S(2)}) %collective-permute-start.6) | collective-permute-done | bytes 24608 | tf_op jit(solution)/shard_map/ppermute | solution.py:617
  27.2 2.3 %shard_map.120 = (f32[4,128,256]{2,1,0:T(8,128)S(1)}, bf16[16,128]{1,0:T(8,128)(2,1)S(1)}) custom-call(bf16[32,384]{1,0:T(8,128)(2,1)S(1)} %shard_map.118.refs_0_, bf16[32,384]{1,0:T(8,128)(2,1)S(1)} %collective-permute-done.5.refs_1_, bf16[32,384]{1,0:T(8,128)(2,1)S(1)} %collective-permute-done.6.refs_2_, ...), custom_call_target="tpu_custom_call" | custom-call | flops 1073741824 | bytes 1048576 | tf_op jit(solution)/shard_map/pallas_call | solution.py:593
  29.6 5.4 %shard_map.121 = (bf16[4096,768]{1,0:T(8,128)(2,1)S(1)}, bf16[2304,128]{1,0:T(8,128)(2,1)S(1)}, bf16[2304,128]{1,0:T(8,128)(2,1)S(1)}, bf16[1,128,256]{2,1,0:T(8...) custom-call(f32[4,128,256]{2,1,0:T(8,128)S(1)} %get-tuple-element.102.spr, ...), custom_call_target="tpu_custom_call" | custom-call | flops 4831838208 | bytes 1048576 | tf_op jit(solution)/shard_map/pallas_call | solution.py:593
  35.0 4.3 %collective-permute-start.12 = (bf16[1,128,256]{2,1,0:T(8,128)(2,1)S(1)}, bf16[1,128,256]{2,1,0:T(8,128)(2,1)S(1)}, u32[]{:S(2)}, u32[]{:S(2)}) collective-permute-start(bf16[1,128,256]{2,1,0:T(8,128)(2,1)S(1)} %get-tuple-element.124), channel_id=1, source_target_pairs={{0,8},{16,24},{8,0},{24,16},{1,9},{17,25},{9,1},{25,17},{2,10},{18... | collective-permute-start | bytes 196616 | tf_op jit(solution)/shard_map/ppermute | solution.py:613
  39.3 0.9 %collective-permute-start.13 = (bf16[1,128,256]{2,1,0:T(8,128)(2,1)S(1)}, bf16[1,128,256]{2,1,0:T(8,128)(2,1)S(1)}, u32[]{:S(2)}, u32[]{:S(2)}) collective-permute-start(bf16[1,128,256]{2,1,0:T(8,128)(2,1)S(1)} %get-tuple-element.125), channel_id=1, source_target_pairs={{8,16},{16,8},{9,17},{17,9},{10,18},{18,10},{11,19},{19,11},{12,20... | collective-permute-start | bytes 196616 | tf_op jit(solution)/shard_map/ppermute | solution.py:613
  40.2 0.3 shard_map.122
  40.5 1.4 %collective-permute-start.9 = (bf16[592,128]{1,0:T(8,128)(2,1)S(1)}, bf16[592,128]{1,0:T(8,128)(2,1)S(1)}, u32[]{:S(2)}, u32[]{:S(2)}) collective-permute-start(bf16[592,128]{1,0:T(8,128)(2,1)S(1)} %get-tuple-element.117), channel_id=1, source_target_pairs={{0,24},{8,16},{16,8},{24,0},{1,25},{9,17},{17,9},{25,1},{2,26},{10... | collective-permute-start | bytes 454664 | tf_op jit(solution)/shard_map/ppermute | solution.py:617
  41.9 2.7 %collective-permute-start.10 = (bf16[592,128]{1,0:T(8,128)(2,1)S(1)}, bf16[592,128]{1,0:T(8,128)(2,1)S(1)}, u32[]{:S(2)}, u32[]{:S(2)}) collective-permute-start(bf16[592,128]{1,0:T(8,128)(2,1)S(1)} %get-tuple-element.118), channel_id=1, source_target_pairs={{0,16},{8,24},{16,0},{24,8},{1,17},{9,25},{17,1},{25,9},{2,18},{10... | collective-permute-start | bytes 454664 | tf_op jit(solution)/shard_map/ppermute | solution.py:617
  44.7 0.1 collective-permute-start.11
  44.8 1.7 %shard_map.123 = (bf16[10,128,256]{2,1,0:T(8,128)(2,1)S(1)}, f32[2,16,256]{2,1,0:T(8,128)S(1)}) custom-call(bf16[4096,768]{1,0:T(8,128)(2,1)S(1)} %get-tuple-element.147.wide, f32[4,128,256]{2,1,0:T(8,128)S(1)} %get-tuple-element.102.spread, bf16[9,256,256]{2,1,0:T(8,128)(2,1)S(1)} %copy-done), custom_call_target="tpu_custom_call" | custom-call | flops 1610612736 | bytes 1048576 | tf_op jit(solution)/shard_map/pallas_call | solution.py:593
  46.7 0.7 collective-permute-start.15
  47.3 0.9 %collective-permute-done.9.refs_1_ = bf16[592,128]{1,0:T(8,128)(2,1)S(1)} collective-permute-done((bf16[592,128]{1,0:T(8,128)(2,1)S(1)}, bf16[592,128]{1,0:T(8,128)(2,1)S(1)}, u32[]{:S(2)}, u32[]{:S(2)}) %collective-permute-start.9) | collective-permute-done | bytes 151584 | tf_op jit(solution)/shard_map/ppermute | solution.py:617
  48.3 2.7 %collective-permute-done.10.refs_2_ = bf16[592,128]{1,0:T(8,128)(2,1)S(1)} collective-permute-done((bf16[592,128]{1,0:T(8,128)(2,1)S(1)}, bf16[592,128]{1,0:T(8,128)(2,1)S(1)}, u32[]{:S(2)}, u32[]{:S(2)}) %collective-permute-start.10) | collective-permute-done | bytes 151584 | tf_op jit(solution)/shard_map/ppermute | solution.py:617
  51.0 1.1 %collective-permute-done.11.refs_3_ = bf16[592,128]{1,0:T(8,128)(2,1)S(1)} collective-permute-done((bf16[592,128]{1,0:T(8,128)(2,1)S(1)}, bf16[592,128]{1,0:T(8,128)(2,1)S(1)}, u32[]{:S(2)}, u32[]{:S(2)}) %collective-permute-start.11) | collective-permute-done | bytes 151584 | tf_op jit(solution)/shard_map/ppermute | solution.py:617
  52.0 0.7 shard_map.124
  52.7 1.8 %collective-permute-start.16 = (bf16[144,128]{1,0:T(8,128)(2,1)S(1)}, bf16[144,128]{1,0:T(8,128)(2,1)S(1)}, u32[]{:S(2)}, u32[]{:S(2)}) collective-permute-start(bf16[144,128]{1,0:T(8,128)(2,1)S(1)} %get-tuple-element.143), channel_id=1, source_target_pairs={{0,6},{2,4},{4,2},{6,0},{1,7},{3,5},{5,3},{7,1},{8,14},{10,12},{12... | collective-permute-start | bytes 110600 | tf_op jit(solution)/shard_map/ppermute | solution.py:617
  54.5 0.3 collective-permute-start.17
  54.8 2.3 %collective-permute-start.18 = (bf16[144,128]{1,0:T(8,128)(2,1)S(1)}, bf16[144,128]{1,0:T(8,128)(2,1)S(1)}, u32[]{:S(2)}, u32[]{:S(2)}) collective-permute-start(bf16[144,128]{1,0:T(8,128)(2,1)S(1)} %get-tuple-element.145), channel_id=1, source_target_pairs={{0,2},{2,0},{4,6},{6,4},{1,3},{3,1},{5,7},{7,5},{8,10},{10,8},{12,... | collective-permute-start | bytes 110600 | tf_op jit(solution)/shard_map/ppermute | solution.py:617
  57.1 1.6 %collective-permute-done.16.refs_1_ = bf16[144,128]{1,0:T(8,128)(2,1)S(1)} collective-permute-done((bf16[144,128]{1,0:T(8,128)(2,1)S(1)}, bf16[144,128]{1,0:T(8,128)(2,1)S(1)}, u32[]{:S(2)}, u32[]{:S(2)}) %collective-permute-start.16) | collective-permute-done | bytes 36896 | tf_op jit(solution)/shard_map/ppermute | solution.py:617
  58.8 1.0 %collective-permute-done.17.refs_2_ = bf16[144,128]{1,0:T(8,128)(2,1)S(1)} collective-permute-done((bf16[144,128]{1,0:T(8,128)(2,1)S(1)}, bf16[144,128]{1,0:T(8,128)(2,1)S(1)}, u32[]{:S(2)}, u32[]{:S(2)}) %collective-permute-start.17) | collective-permute-done | bytes 36896 | tf_op jit(solution)/shard_map/ppermute | solution.py:617
  59.8 2.1 %collective-permute-start.21 = (bf16[144,128]{1,0:T(8,128)(2,1)S(1)}, bf16[144,128]{1,0:T(8,128)(2,1)S(1)}, u32[]{:S(2)}, u32[]{:S(2)}) collective-permute-start(bf16[144,128]{1,0:T(8,128)(2,1)S(1)} %shard_map.126.refs_0_), channel_id=1, source_target_pairs={{0,6},{2,4},{4,2},{6,0},{1,7},{3,5},{5,3},{7,1},{8,14},{10,12},{12... | collective-permute-start | bytes 110600 | tf_op jit(solution)/shard_map/ppermute | solution.py:617
  61.9 0.7 collective-permute-start.20
  62.6 1.6 %collective-permute-start.19 = (bf16[144,128]{1,0:T(8,128)(2,1)S(1)}, bf16[144,128]{1,0:T(8,128)(2,1)S(1)}, u32[]{:S(2)}, u32[]{:S(2)}) collective-permute-start(bf16[144,128]{1,0:T(8,128)(2,1)S(1)} %shard_map.126.refs_0_), channel_id=1, source_target_pairs={{0,2},{2,0},{4,6},{6,4},{1,3},{3,1},{5,7},{7,5},{8,10},{10,8},{12,... | collective-permute-start | bytes 110600 | tf_op jit(solution)/shard_map/ppermute | solution.py:617
  64.2 1.4 %collective-permute-done.21.refs_3_ = bf16[144,128]{1,0:T(8,128)(2,1)S(1)} collective-permute-done((bf16[144,128]{1,0:T(8,128)(2,1)S(1)}, bf16[144,128]{1,0:T(8,128)(2,1)S(1)}, u32[]{:S(2)}, u32[]{:S(2)}) %collective-permute-start.21) | collective-permute-done | bytes 36896 | tf_op jit(solution)/shard_map/ppermute | solution.py:617
  65.6 1.3 %collective-permute-done.20.refs_2_ = bf16[144,128]{1,0:T(8,128)(2,1)S(1)} collective-permute-done((bf16[144,128]{1,0:T(8,128)(2,1)S(1)}, bf16[144,128]{1,0:T(8,128)(2,1)S(1)}, u32[]{:S(2)}, u32[]{:S(2)}) %collective-permute-start.20) | collective-permute-done | bytes 36896 | tf_op jit(solution)/shard_map/ppermute | solution.py:617
  66.9 0.1 collective-permute-done.19.refs_1_
  67.0 1.4 %collective-permute-start.24 = (bf16[4,144,128]{2,1,0:T(8,128)(2,1)S(1)}, bf16[4,144,128]{2,1,0:T(8,128)(2,1)S(1)}, u32[]{:S(2)}, u32[]{:S(2)}) collective-permute-start(bf16[4,144,128]{2,1,0:T(8,128)(2,1)S(1)} %shard_map.127.refs_0_), channel_id=1, source_target_pairs={{0,24},{8,16},{16,8},{24,0},{1,25},{9,17},{17,9},{25,1},{2,26},{10... | collective-permute-start | bytes 442376 | tf_op jit(solution)/shard_map/ppermute | solution.py:617
  68.4 1.5 %collective-permute-start.23 = (bf16[4,144,128]{2,1,0:T(8,128)(2,1)S(1)}, bf16[4,144,128]{2,1,0:T(8,128)(2,1)S(1)}, u32[]{:S(2)}, u32[]{:S(2)}) collective-permute-start(bf16[4,144,128]{2,1,0:T(8,128)(2,1)S(1)} %shard_map.127.refs_0_), channel_id=1, source_target_pairs={{0,16},{8,24},{16,0},{24,8},{1,17},{9,25},{17,1},{25,9},{2,18},{10... | collective-permute-start | bytes 442376 | tf_op jit(solution)/shard_map/ppermute | solution.py:617
  69.8 0.7 collective-permute-start.22
  70.6 4.7 %shard_map.128 = bf16[32,128,256]{2,1,0:T(8,128)(2,1)} custom-call(bf16[4096,768]{1,0:T(8,128)(2,1)S(1)} %get-tuple-element.147.wide, bf16[1,128,256]{2,1,0:T(8,128)(2,1)S(1)} %get-tuple-element.148.top, bf16[1,128,256]{2,1,0:T(8,128)(2,1)S(1)} %get-tuple-element.149.bot, bf16[48,256]{1,0:T(8,128)(2,1)S(1)} %collective-permute-done.14.even, ...), custom_call_target="tpu_custom_call" | custom-call | flops 2415919104 | bytes 1048576 | tf_op jit(solution)/shard_map/pallas_call | solution.py:593
  75.4 1.1 %shard_map.130.refs_1_ = f32[2304,256]{1,0:T(8,128)} custom-call(bf16[4,4,144,128]{3,2,1,0:T(8,128)(2,1)S(1)} %shard_map.129.refs_0_), custom_call_target="tpu_custom_call" | custom-call | flops 1048576 | bytes 1048576 | tf_op jit(solution)/shard_map/pallas_call | solution.py:593
  76.5 0.9 %collective-permute-done.25.refs_0_ = bf16[4,4,144,128]{3,2,1,0:T(8,128)(2,1)S(1)} collective-permute-done((bf16[4,4,144,128]{3,2,1,0:T(8,128)(2,1)S(1)}, bf16[4,4,144,128]{3,2,1,0:T(8,128)(2,1)S(1)}, u32[]{:S(2)}, u32[]{:S(2)}) %collective-permute-start.25) | collective-permute-done | bytes 589856 | tf_op jit(solution)/shard_map/ppermute | solution.py:779
  77.4 1.1 %shard_map.131 = f32[2304,256]{1,0:T(8,128)} custom-call(bf16[4,4,144,128]{3,2,1,0:T(8,128)(2,1)S(1)} %collective-permute-done.25.refs_0_, f32[2304,256]{1,0:T(8,128)} %shard_map.130.refs_1_), custom_call_target="tpu_custom_call", output_to_operand_aliasing={{}: (1, {})} | custom-call | flops 1048576 | bytes 1048576 | tf_op jit(solution)/shard_map/pallas_call | solution.py:593
  (43 shorter events, 0.6 us)
Async XLA Ops:
  1.5 3.7 %copy-start = (bf16[9,256,256]{2,1,0:T(8,128)(2,1)S(1)}, bf16[9,256,256]{2,1,0:T(8,128)(2,1)}, u32[]{:S(2)}) copy-start(bf16[9,256,256]{2,1,0:T(8,128)(2,1)} %weight.5) | copy-start | bytes 3538948
  1.5 3.7 %copy-start.1 = (bf16[32,128,256]{2,1,0:T(8,128)(2,1)S(1)}, bf16[32,128,256]{2,1,0:T(8,128)(2,1)}, u32[]{:S(2)}) copy-start(bf16[32,128,256]{2,1,0:T(8,128)(2,1)} %feat.3) | copy-start | bytes 6291460
  1.5 3.7 %copy-start.3 = (s32[2,8]{1,0:T(2,128)S(1)}, s32[2,8]{1,0:T(2,128)}, u32[]{:S(2)}) copy-start(s32[2,8]{1,0:T(2,128)} %flags_ref.1) | copy-start | bytes 196
  1.6 7.4 %collective-permute-start = (bf16[1,128,256]{2,1,0:T(8,128)(2,1)S(1)}, bf16[1,128,256]{2,1,0:T(8,128)(2,1)S(1)}, u32[]{:S(2)}, u32[]{:S(2)}) collective-permute-start(bf16[1,128,256]{2,1,0:T(8,128)(2,1)S(1)} %get-tuple-element.84), channel_id=1, source_target_pairs={{0,8},{16,24},{8,0},{24,16},{1,9},{17,25},{9,1},{25,17},{2,10},{18... | collective-permute-start | bytes 196616 | tf_op jit(solution)/shard_map/ppermute | solution.py:613
  4.6 4.4 %collective-permute-start.1 = (bf16[1,128,256]{2,1,0:T(8,128)(2,1)S(1)}, bf16[1,128,256]{2,1,0:T(8,128)(2,1)S(1)}, u32[]{:S(2)}, u32[]{:S(2)}) collective-permute-start(bf16[1,128,256]{2,1,0:T(8,128)(2,1)S(1)} %get-tuple-element.85), channel_id=1, source_target_pairs={{8,16},{16,8},{9,17},{17,9},{10,18},{18,10},{11,19},{19,11},{12,20... | collective-permute-start | bytes 196616 | tf_op jit(solution)/shard_map/ppermute | solution.py:613
  9.1 4.6 %collective-permute-start.2 = (bf16[48,256]{1,0:T(8,128)(2,1)S(1)}, bf16[48,256]{1,0:T(8,128)(2,1)S(1)}, u32[]{:S(2)}, u32[]{:S(2)}) collective-permute-start(bf16[48,256]{1,0:T(8,128)(2,1)S(1)} %get-tuple-element.96), channel_id=1, source_target_pairs={{0,1},{2,3},{4,5},{6,7},{1,0},{3,2},{5,4},{7,6},{8,9},{10,11},{12,... | collective-permute-start | bytes 73736 | tf_op jit(solution)/shard_map/ppermute | solution.py:613
  9.2 4.6 %copy-start.2 = (bf16[4,256,256]{2,1,0:T(8,128)(2,1)S(1)}, bf16[4,256,256]{2,1,0:T(8,128)(2,1)}, u32[]{:S(2)}) copy-start(bf16[4,256,256]{2,1,0:T(8,128)(2,1)} %refs_8_.1) | copy-start | bytes 1572868
  9.2 4.6 %copy-start.4 = (s32[1,1,16,1]{2,3,1,0:T(1,128)S(1)}, s32[1,1,16,1]{2,3,1,0:T(1,128)}, u32[]{:S(2)}) copy-start(s32[1,1,16,1]{2,3,1,0:T(1,128)} %param.11) | copy-start | bytes 196
  9.2 4.5 %collective-permute-start.3 = (bf16[48,256]{1,0:T(8,128)(2,1)S(1)}, bf16[48,256]{1,0:T(8,128)(2,1)S(1)}, u32[]{:S(2)}, u32[]{:S(2)}) collective-permute-start(bf16[48,256]{1,0:T(8,128)(2,1)S(1)} %get-tuple-element.97), channel_id=1, source_target_pairs={{1,2},{3,4},{5,6},{2,1},{4,3},{6,5},{9,10},{11,12},{13,14},{10,9},... | collective-permute-start | bytes 73736 | tf_op jit(solution)/shard_map/ppermute | solution.py:613
  13.7 10.2 %copy-start.5 = (f32[256,256]{1,0:T(8,128)S(1)}, f32[256,256]{1,0:T(8,128)}, u32[]{:S(2)}) copy-start(f32[256,256]{1,0:T(8,128)} %w_query.1) | copy-start | bytes 786436
  13.8 10.2 %copy-start.6 = (f32[256,256]{1,0:T(8,128)S(1)}, f32[256,256]{1,0:T(8,128)}, u32[]{:S(2)}) copy-start(f32[256,256]{1,0:T(8,128)} %w_key.1) | copy-start | bytes 786436
  13.8 10.2 %copy-start.7 = (f32[256,256]{1,0:T(8,128)S(1)}, f32[256,256]{1,0:T(8,128)}, u32[]{:S(2)}) copy-start(f32[256,256]{1,0:T(8,128)} %w_value.1) | copy-start | bytes 786436
  15.8 3.8 %collective-permute-start.4 = (bf16[16,384]{1,0:T(8,128)(2,1)S(1)}, bf16[16,384]{1,0:T(8,128)(2,1)S(1)}, u32[]{:S(2)}, u32[]{:S(2)}) collective-permute-start(bf16[16,384]{1,0:T(8,128)(2,1)S(1)} %get-tuple-element.98.one.token), channel_id=1, source_target_pairs={{0,1},{1,0},{2,3},{3,2},{4,5},{5,4},{6,7},{7,6},{8,9},{9,8},{10,11... | collective-permute-start | bytes 36872 | tf_op jit(solution)/shard_map/ppermute | solution.py:680
  19.6 7.6 %copy-start.8 = (f32[256]{0:T(256)S(1)}, f32[256]{0:T(256)}, u32[]{:S(2)}) copy-start(f32[256]{0:T(256)} %param.17) | copy-start | bytes 3076
  19.6 5.6 %collective-permute-start.7 = (bf16[32,384]{1,0:T(8,128)(2,1)S(1)}, bf16[32,384]{1,0:T(8,128)(2,1)S(1)}, u32[]{:S(2)}, u32[]{:S(2)}) collective-permute-start(bf16[32,384]{1,0:T(8,128)(2,1)S(1)} %shard_map.118.refs_0_), channel_id=1, source_target_pairs={{0,6},{2,4},{4,2},{6,0},{1,7},{3,5},{5,3},{7,1},{8,14},{10,12},{12... | collective-permute-start | bytes 73736 | tf_op jit(solution)/shard_map/ppermute | solution.py:617
  22.4 4.8 %collective-permute-start.6 = (bf16[32,384]{1,0:T(8,128)(2,1)S(1)}, bf16[32,384]{1,0:T(8,128)(2,1)S(1)}, u32[]{:S(2)}, u32[]{:S(2)}) collective-permute-start(bf16[32,384]{1,0:T(8,128)(2,1)S(1)} %shard_map.118.refs_0_), channel_id=1, source_target_pairs={{0,4},{2,6},{4,0},{6,2},{1,5},{3,7},{5,1},{7,3},{8,12},{10,14},{12... | collective-permute-start | bytes 73736 | tf_op jit(solution)/shard_map/ppermute | solution.py:617
  22.6 4.6 %collective-permute-start.5 = (bf16[32,384]{1,0:T(8,128)(2,1)S(1)}, bf16[32,384]{1,0:T(8,128)(2,1)S(1)}, u32[]{:S(2)}, u32[]{:S(2)}) collective-permute-start(bf16[32,384]{1,0:T(8,128)(2,1)S(1)} %shard_map.118.refs_0_), channel_id=1, source_target_pairs={{0,2},{2,0},{4,6},{6,4},{1,3},{3,1},{5,7},{7,5},{8,10},{10,8},{12,... | collective-permute-start | bytes 73736 | tf_op jit(solution)/shard_map/ppermute | solution.py:617
  34.9 5.3 %collective-permute-start.8 = (bf16[2304,128]{1,0:T(8,128)(2,1)S(1)}, bf16[2304,128]{1,0:T(8,128)(2,1)S(1)}, u32[]{:S(2)}, u32[]{:S(2)}) collective-permute-start(bf16[2304,128]{1,0:T(8,128)(2,1)S(1)} %get-tuple-element.109), channel_id=1, source_target_pairs={{0,1},{1,0},{2,3},{3,2},{4,5},{5,4},{6,7},{7,6},{8,9},{9,8},{10,11... | collective-permute-start | bytes 1769480 | tf_op jit(solution)/shard_map/ppermute | solution.py:719
  35.0 11.5 %collective-permute-start.12 = (bf16[1,128,256]{2,1,0:T(8,128)(2,1)S(1)}, bf16[1,128,256]{2,1,0:T(8,128)(2,1)S(1)}, u32[]{:S(2)}, u32[]{:S(2)}) collective-permute-start(bf16[1,128,256]{2,1,0:T(8,128)(2,1)S(1)} %get-tuple-element.124), channel_id=1, source_target_pairs={{0,8},{16,24},{8,0},{24,16},{1,9},{17,25},{9,1},{25,17},{2,10},{18... | collective-permute-start | bytes 196616 | tf_op jit(solution)/shard_map/ppermute | solution.py:613
  39.3 7.2 %collective-permute-start.13 = (bf16[1,128,256]{2,1,0:T(8,128)(2,1)S(1)}, bf16[1,128,256]{2,1,0:T(8,128)(2,1)S(1)}, u32[]{:S(2)}, u32[]{:S(2)}) collective-permute-start(bf16[1,128,256]{2,1,0:T(8,128)(2,1)S(1)} %get-tuple-element.125), channel_id=1, source_target_pairs={{8,16},{16,8},{9,17},{17,9},{10,18},{18,10},{11,19},{19,11},{12,20... | collective-permute-start | bytes 196616 | tf_op jit(solution)/shard_map/ppermute | solution.py:613
  40.5 7.7 %collective-permute-start.9 = (bf16[592,128]{1,0:T(8,128)(2,1)S(1)}, bf16[592,128]{1,0:T(8,128)(2,1)S(1)}, u32[]{:S(2)}, u32[]{:S(2)}) collective-permute-start(bf16[592,128]{1,0:T(8,128)(2,1)S(1)} %get-tuple-element.117), channel_id=1, source_target_pairs={{0,24},{8,16},{16,8},{24,0},{1,25},{9,17},{17,9},{25,1},{2,26},{10... | collective-permute-start | bytes 454664 | tf_op jit(solution)/shard_map/ppermute | solution.py:617
  41.9 9.1 %collective-permute-start.10 = (bf16[592,128]{1,0:T(8,128)(2,1)S(1)}, bf16[592,128]{1,0:T(8,128)(2,1)S(1)}, u32[]{:S(2)}, u32[]{:S(2)}) collective-permute-start(bf16[592,128]{1,0:T(8,128)(2,1)S(1)} %get-tuple-element.118), channel_id=1, source_target_pairs={{0,16},{8,24},{16,0},{24,8},{1,17},{9,25},{17,1},{25,9},{2,18},{10... | collective-permute-start | bytes 454664 | tf_op jit(solution)/shard_map/ppermute | solution.py:617
  44.7 7.4 %collective-permute-start.11 = (bf16[592,128]{1,0:T(8,128)(2,1)S(1)}, bf16[592,128]{1,0:T(8,128)(2,1)S(1)}, u32[]{:S(2)}, u32[]{:S(2)}) collective-permute-start(bf16[592,128]{1,0:T(8,128)(2,1)S(1)} %get-tuple-element.119), channel_id=1, source_target_pairs={{0,8},{8,0},{16,24},{24,16},{1,9},{9,1},{17,25},{25,17},{2,10},{10... | collective-permute-start | bytes 454664 | tf_op jit(solution)/shard_map/ppermute | solution.py:617
  46.6 6.1 %collective-permute-start.14 = (bf16[48,256]{1,0:T(8,128)(2,1)S(1)}, bf16[48,256]{1,0:T(8,128)(2,1)S(1)}, u32[]{:S(2)}, u32[]{:S(2)}) collective-permute-start(bf16[48,256]{1,0:T(8,128)(2,1)S(1)} %get-tuple-element.140), channel_id=1, source_target_pairs={{0,1},{2,3},{4,5},{6,7},{1,0},{3,2},{5,4},{7,6},{8,9},{10,11},{12,... | collective-permute-start | bytes 73736 | tf_op jit(solution)/shard_map/ppermute | solution.py:613
  46.7 6.1 %collective-permute-start.15 = (bf16[48,256]{1,0:T(8,128)(2,1)S(1)}, bf16[48,256]{1,0:T(8,128)(2,1)S(1)}, u32[]{:S(2)}, u32[]{:S(2)}) collective-permute-start(bf16[48,256]{1,0:T(8,128)(2,1)S(1)} %get-tuple-element.141), channel_id=1, source_target_pairs={{1,2},{3,4},{5,6},{2,1},{4,3},{6,5},{9,10},{11,12},{13,14},{10,9},... | collective-permute-start | bytes 73736 | tf_op jit(solution)/shard_map/ppermute | solution.py:613
  52.7 6.0 %collective-permute-start.16 = (bf16[144,128]{1,0:T(8,128)(2,1)S(1)}, bf16[144,128]{1,0:T(8,128)(2,1)S(1)}, u32[]{:S(2)}, u32[]{:S(2)}) collective-permute-start(bf16[144,128]{1,0:T(8,128)(2,1)S(1)} %get-tuple-element.143), channel_id=1, source_target_pairs={{0,6},{2,4},{4,2},{6,0},{1,7},{3,5},{5,3},{7,1},{8,14},{10,12},{12... | collective-permute-start | bytes 110600 | tf_op jit(solution)/shard_map/ppermute | solution.py:617
  54.5 5.3 %collective-permute-start.17 = (bf16[144,128]{1,0:T(8,128)(2,1)S(1)}, bf16[144,128]{1,0:T(8,128)(2,1)S(1)}, u32[]{:S(2)}, u32[]{:S(2)}) collective-permute-start(bf16[144,128]{1,0:T(8,128)(2,1)S(1)} %get-tuple-element.144), channel_id=1, source_target_pairs={{0,4},{2,6},{4,0},{6,2},{1,5},{3,7},{5,1},{7,3},{8,12},{10,14},{12... | collective-permute-start | bytes 110600 | tf_op jit(solution)/shard_map/ppermute | solution.py:617
  54.8 5.0 %collective-permute-start.18 = (bf16[144,128]{1,0:T(8,128)(2,1)S(1)}, bf16[144,128]{1,0:T(8,128)(2,1)S(1)}, u32[]{:S(2)}, u32[]{:S(2)}) collective-permute-start(bf16[144,128]{1,0:T(8,128)(2,1)S(1)} %get-tuple-element.145), channel_id=1, source_target_pairs={{0,2},{2,0},{4,6},{6,4},{1,3},{3,1},{5,7},{7,5},{8,10},{10,8},{12,... | collective-permute-start | bytes 110600 | tf_op jit(solution)/shard_map/ppermute | solution.py:617
  59.8 5.8 %collective-permute-start.21 = (bf16[144,128]{1,0:T(8,128)(2,1)S(1)}, bf16[144,128]{1,0:T(8,128)(2,1)S(1)}, u32[]{:S(2)}, u32[]{:S(2)}) collective-permute-start(bf16[144,128]{1,0:T(8,128)(2,1)S(1)} %shard_map.126.refs_0_), channel_id=1, source_target_pairs={{0,6},{2,4},{4,2},{6,0},{1,7},{3,5},{5,3},{7,1},{8,14},{10,12},{12... | collective-permute-start | bytes 110600 | tf_op jit(solution)/shard_map/ppermute | solution.py:617
  61.9 5.0 %collective-permute-start.20 = (bf16[144,128]{1,0:T(8,128)(2,1)S(1)}, bf16[144,128]{1,0:T(8,128)(2,1)S(1)}, u32[]{:S(2)}, u32[]{:S(2)}) collective-permute-start(bf16[144,128]{1,0:T(8,128)(2,1)S(1)} %shard_map.126.refs_0_), channel_id=1, source_target_pairs={{0,4},{2,6},{4,0},{6,2},{1,5},{3,7},{5,1},{7,3},{8,12},{10,14},{12... | collective-permute-start | bytes 110600 | tf_op jit(solution)/shard_map/ppermute | solution.py:617
  62.6 4.4 %collective-permute-start.19 = (bf16[144,128]{1,0:T(8,128)(2,1)S(1)}, bf16[144,128]{1,0:T(8,128)(2,1)S(1)}, u32[]{:S(2)}, u32[]{:S(2)}) collective-permute-start(bf16[144,128]{1,0:T(8,128)(2,1)S(1)} %shard_map.126.refs_0_), channel_id=1, source_target_pairs={{0,2},{2,0},{4,6},{6,4},{1,3},{3,1},{5,7},{7,5},{8,10},{10,8},{12,... | collective-permute-start | bytes 110600 | tf_op jit(solution)/shard_map/ppermute | solution.py:617
  67.0 8.2 %collective-permute-start.24 = (bf16[4,144,128]{2,1,0:T(8,128)(2,1)S(1)}, bf16[4,144,128]{2,1,0:T(8,128)(2,1)S(1)}, u32[]{:S(2)}, u32[]{:S(2)}) collective-permute-start(bf16[4,144,128]{2,1,0:T(8,128)(2,1)S(1)} %shard_map.127.refs_0_), channel_id=1, source_target_pairs={{0,24},{8,16},{16,8},{24,0},{1,25},{9,17},{17,9},{25,1},{2,26},{10... | collective-permute-start | bytes 442376 | tf_op jit(solution)/shard_map/ppermute | solution.py:617
  68.4 6.9 %collective-permute-start.23 = (bf16[4,144,128]{2,1,0:T(8,128)(2,1)S(1)}, bf16[4,144,128]{2,1,0:T(8,128)(2,1)S(1)}, u32[]{:S(2)}, u32[]{:S(2)}) collective-permute-start(bf16[4,144,128]{2,1,0:T(8,128)(2,1)S(1)} %shard_map.127.refs_0_), channel_id=1, source_target_pairs={{0,16},{8,24},{16,0},{24,8},{1,17},{9,25},{17,1},{25,9},{2,18},{10... | collective-permute-start | bytes 442376 | tf_op jit(solution)/shard_map/ppermute | solution.py:617
  69.8 5.4 %collective-permute-start.22 = (bf16[4,144,128]{2,1,0:T(8,128)(2,1)S(1)}, bf16[4,144,128]{2,1,0:T(8,128)(2,1)S(1)}, u32[]{:S(2)}, u32[]{:S(2)}) collective-permute-start(bf16[4,144,128]{2,1,0:T(8,128)(2,1)S(1)} %shard_map.127.refs_0_), channel_id=1, source_target_pairs={{0,8},{8,0},{16,24},{24,16},{1,9},{9,1},{17,25},{25,17},{2,10},{10... | collective-permute-start | bytes 442376 | tf_op jit(solution)/shard_map/ppermute | solution.py:617
  75.3 2.1 %collective-permute-start.25 = (bf16[4,4,144,128]{3,2,1,0:T(8,128)(2,1)S(1)}, bf16[4,4,144,128]{3,2,1,0:T(8,128)(2,1)S(1)}, u32[]{:S(2)}, u32[]{:S(2)}) collective-permute-start(bf16[4,4,144,128]{3,2,1,0:T(8,128)(2,1)S(1)} %shard_map.129.refs_0_), channel_id=1, source_target_pairs={{0,1},{1,0},{2,3},{3,2},{4,5},{5,4},{6,7},{7,6},{8,9},{9,8},{10,11... | collective-permute-start | bytes 1769480 | tf_op jit(solution)/shard_map/ppermute | solution.py:779
